TPU v7x, 512 devices: a whole 4x8x8 slice. The times are simulated.
512 devices in a mesh: dp: 4 (over y_lo, core), head: 8 (over z), ctx: 16 (over x, y_hi).
Axes of the slice: x: 4, y: 8 (y_hi: 4, y_lo: 2; y = y_hi * 2 + y_lo), z: 8, core: 2. Of those that a mesh axis runs over, the one named last changes fastest.
Arguments:
- slab_order: int32 [128], P('dp'), parts along dimension 0, may hold values from 0 to 31, each once
- doc_ids: int32 [8192], P('dp'), parts along dimension 0, may hold values from 0 to 3, never falling along the last dimension, each value on 1 to 1024 neighbouring positions
- query_first: bfloat16 [8192, 6144], P(('dp', 'ctx'), 'head'), parts along dimension 0, may hold values from -12 to 12
- query_second: bfloat16 [8192, 6144], P(('dp', 'ctx'), 'head'), parts along dimension 0, may hold values from -12 to 12
- shared_keys: bfloat16 [8192, 1024], P(('dp', 'ctx'), 'head'), parts along dimension 0, may hold values from -4 to 4
- shared_values: bfloat16 [8192, 1024], P(('dp', 'ctx'), 'head'), parts along dimension 0, may hold values from -6 to 6
- out_grad_first: bfloat16 [8192, 6144], P(('dp', 'ctx'), 'head'), parts along dimension 0, may hold values from -6 to 6
- out_grad_second: bfloat16 [8192, 6144], P(('dp', 'ctx'), 'head'), parts along dimension 0, may hold values from -6 to 6
Outputs:
- query_grad_first: bfloat16 [8192, 6144], P(('dp', 'ctx'), 'head'), parts along dimension 0
- query_grad_second: bfloat16 [8192, 6144], P(('dp', 'ctx'), 'head'), parts along dimension 0
- key_grad: bfloat16 [8192, 1024], P(('dp', 'ctx'), 'head'), parts along dimension 0
- value_grad: bfloat16 [8192, 1024], P(('dp', 'ctx'), 'head'), parts along dimension 0
There are 4 independent parts, one for each index of `dp`. A program takes and returns all parts, laid end to end along the dimension named above; each array names one. Nothing has to cross between parts.
Inputs may be any that keep to these rules, and one draw needn't show every extreme that they name: `slab_order`: every slab number appears exactly once. `doc_ids`: document numbers never fall along the positions; each of the 4 numbers names one run of 1 to 1024 positions, one run of exactly 1024.
All inputs are finite; a program needn't handle non-finite values.
Results may differ from a plain program's by a relative error of at most 0.034.
Values may be sent and summed in bfloat16 or wider, within the bound.
No kernel may reach another device: no remote copies, remote signals or barrier semaphores. Data moves between devices by JAX's collectives and lax.ppermute only.
A program may use at most 64 MiB of HBM per device.

v0:
```python
import math

import jax
import jax.numpy as jnp
from jax import lax
from jax.sharding import PartitionSpec as P

HD = 128


MASKED_SCORE = -1e30


def storage_layout(slab_order, doc_ids, total_rows):
    slab_rows = total_rows // slab_order.shape[0]
    within = jnp.arange(slab_rows, dtype=jnp.int32)
    positions = (slab_order[:, None] * slab_rows + within[None, :]).reshape(total_rows)
    return (positions, jnp.take(doc_ids, positions, axis=0))


def in_blocks(fold_keys, carried, block_pair):
    key_count = block_pair[0].shape[0]
    step_rows = math.gcd(key_count, 512)

    def advance(step_id, running):
        offset = step_id * step_rows
        window = tuple(
            (lax.dynamic_slice_in_dim(member, offset, step_rows, 0) for member in block_pair)
        )
        return fold_keys(running, window, offset)

    return lax.fori_loop(0, key_count // step_rows, advance, carried)


def per_device(
    slab_order,
    doc_ids,
    query_first,
    query_second,
    shared_keys,
    shared_values,
    out_grad_first,
    out_grad_second,
):
    row_count = shared_keys.shape[0]
    head_count = query_first.shape[1] // HD
    total_rows = row_count * lax.axis_size("ctx")
    positions, documents = storage_layout(slab_order, doc_ids, total_rows)
    own_start = lax.axis_index("ctx") * row_count
    own_pos = lax.dynamic_slice_in_dim(positions, own_start, row_count)
    own_doc = lax.dynamic_slice_in_dim(documents, own_start, row_count)
    softmax_scale = 1.0 / math.sqrt(HD)
    queries = (
        query_first.reshape(row_count, head_count, HD),
        query_second.reshape(row_count, head_count, HD),
    )
    cotangents = (
        out_grad_first.reshape(row_count, head_count, HD),
        out_grad_second.reshape(row_count, head_count, HD),
    )

    def visible(row_start, key_count):
        key_pos = lax.dynamic_slice_in_dim(positions, row_start, key_count)
        key_doc = lax.dynamic_slice_in_dim(documents, row_start, key_count)
        return (key_pos[None, :] <= own_pos[:, None]) & (key_doc[None, :] == own_doc[:, None])

    def forward_fold(chosen):

        def fold_keys(carried, block_pair, row_start):
            key_block, value_block = block_pair
            allowed = visible(row_start, key_block.shape[0])
            value_wide = value_block.astype(jnp.float32)

            def compute(running):
                updated = []
                for slot_id, layer_id in enumerate(chosen):
                    partial_sum, row_top, row_total = running[slot_id]
                    scores = softmax_scale * jnp.einsum(
                        "rhd,nd->hrn",
                        queries[layer_id],
                        key_block,
                        preferred_element_type=jnp.float32,
                    )
                    masked = jnp.where(allowed[None], scores, MASKED_SCORE)
                    new_top = jnp.maximum(row_top, jnp.max(masked, axis=-1))
                    weights = jnp.where(allowed[None], jnp.exp(masked - new_top[..., None]), 0.0)
                    factor = jnp.exp(row_top - new_top)
                    partial_sum = partial_sum * factor[..., None] + jnp.einsum(
                        "hrn,nd->hrd", weights, value_wide, precision=lax.Precision.HIGHEST
                    )
                    row_total = row_total * factor + jnp.sum(weights, axis=-1)
                    updated.append((partial_sum, new_top, row_total))
                return tuple(updated)

            return compute(carried)

        return fold_keys

    layer_plans = ((0,), (1,))
    log_totals = [None, None]
    offsets = [None, None]
    for chosen in layer_plans:
        initial = tuple(
            (
                (
                    jnp.zeros((head_count, row_count, HD), jnp.float32),
                    jnp.full((head_count, row_count), MASKED_SCORE, jnp.float32),
                    jnp.zeros((head_count, row_count), jnp.float32),
                )
                for layer_id in chosen
            )
        )
        final_state = in_blocks(
            forward_fold(chosen),
            initial,
            (
                lax.all_gather(shared_keys, "ctx", axis=0, tiled=True),
                lax.all_gather(shared_values, "ctx", axis=0, tiled=True),
            ),
        )
        for slot_id, layer_id in enumerate(chosen):
            partial_sum, row_top, row_total = final_state[slot_id]
            attended = (partial_sum / row_total[..., None]).astype(jnp.bfloat16)
            log_totals[layer_id] = row_top + jnp.log(row_total)
            offsets[layer_id] = jnp.einsum(
                "rhd,hrd->hr", cotangents[layer_id], attended, preferred_element_type=jnp.float32
            )

    def backward_fold(chosen):

        def fold_keys(carried, block_pair, row_start):
            key_block, value_block = block_pair
            key_count = key_block.shape[0]
            allowed = visible(row_start, key_count)

            def compute(running):
                query_terms, key_terms = running
                key_part = jnp.zeros((key_count, HD), jnp.float32)
                value_part = jnp.zeros((key_count, HD), jnp.float32)
                updated = []
                for slot_id, layer_id in enumerate(chosen):
                    scores = softmax_scale * jnp.einsum(
                        "rhd,nd->hrn",
                        queries[layer_id],
                        key_block,
                        preferred_element_type=jnp.float32,
                    )
                    weights = jnp.where(
                        allowed[None], jnp.exp(scores - log_totals[layer_id][..., None]), 0.0
                    )
                    weights_low = weights.astype(jnp.bfloat16)
                    weight_grad = jnp.einsum(
                        "rhd,nd->hrn",
                        cotangents[layer_id],
                        value_block,
                        preferred_element_type=jnp.float32,
                    )
                    score_grad = (weights * (weight_grad - offsets[layer_id][..., None])).astype(
                        jnp.bfloat16
                    )
                    updated.append(
                        query_terms[slot_id]
                        + softmax_scale
                        * jnp.einsum(
                            "hrn,nd->rhd", score_grad, key_block, preferred_element_type=jnp.float32
                        )
                    )
                    key_part = softmax_scale * jnp.einsum(
                        "hrn,rhd->nd",
                        score_grad,
                        queries[layer_id],
                        preferred_element_type=jnp.float32,
                    )
                    value_part = jnp.einsum(
                        "hrn,rhd->nd",
                        weights_low,
                        cotangents[layer_id],
                        preferred_element_type=jnp.float32,
                    )
                current = lax.dynamic_slice_in_dim(key_terms, row_start, key_count, 0)
                key_terms = lax.dynamic_update_slice_in_dim(
                    key_terms,
                    current + jnp.concatenate([key_part, value_part], axis=1),
                    row_start,
                    0,
                )
                return (tuple(updated), key_terms)

            return compute(carried)

        return fold_keys

    key_terms = jnp.zeros((total_rows, 2 * HD), jnp.float32)
    query_terms = [None, None]
    for chosen in layer_plans:
        initial = (
            tuple((jnp.zeros((row_count, head_count, HD), jnp.float32) for layer_id in chosen)),
            key_terms,
        )
        finished, key_terms = in_blocks(
            backward_fold(chosen),
            initial,
            (
                lax.all_gather(shared_keys, "ctx", axis=0, tiled=True),
                lax.all_gather(shared_values, "ctx", axis=0, tiled=True),
            ),
        )
        for slot_id, layer_id in enumerate(chosen):
            query_terms[layer_id] = (
                finished[slot_id].reshape(row_count, head_count * HD).astype(jnp.bfloat16)
            )
    summed = lax.psum_scatter(
        key_terms.astype(jnp.bfloat16), "ctx", scatter_dimension=0, tiled=True
    ).astype(jnp.float32)
    return (
        query_terms[0],
        query_terms[1],
        summed[:, :HD].astype(jnp.bfloat16),
        summed[:, HD:].astype(jnp.bfloat16),
    )


def solution(mesh):
    in_specs = (
        P("dp"),
        P("dp"),
        P(("dp", "ctx"), "head"),
        P(("dp", "ctx"), "head"),
        P(("dp", "ctx"), "head"),
        P(("dp", "ctx"), "head"),
        P(("dp", "ctx"), "head"),
        P(("dp", "ctx"), "head"),
    )
    out_specs = (
        P(("dp", "ctx"), "head"),
        P(("dp", "ctx"), "head"),
        P(("dp", "ctx"), "head"),
        P(("dp", "ctx"), "head"),
    )
    return jax.shard_map(
        per_device, mesh=mesh, in_specs=in_specs, out_specs=out_specs, check_vma=False
    )
```

profile of v0, /device:TPU:448, one launch (start us, length us, event | category | flops | bytes accessed | tf_op | source)
XLA Modules:
  0.0 298.8 jit_solution(12313309076967424212)
XLA Ops:
  8.2 48.6 %all_gather.4 = bf16[2048,128]{1,0:T(8,128)(2,1)S(1)} all-gather(bf16[128,128]{1,0:T(8,128)(2,1)} %param.20), channel_id=1, replica_groups=mesh['dp'=4,'head'=8,'ctx'=16] {'ctx'}, dimensions={0}, use_global_device_ids=true | all-gather | bytes 557056 | tf_op jit(solution)/shard_map/all_gather | solution.py:204
  56.9 11.8 %gather_fusion = s32[2048]{0:T(1024)S(1)} fusion(s32[2048]{0:T(1024)S(1)} %copy-done, s32[2048]{0:T(1024)S(1)} %broadcast_clamp_fusion), kind=kCustom, calls=%fused_computation | custom fusion | bytes 24576 | tf_op jit(solution)/shard_map/jit(_take)/gather | solution.py:18
  69.1 44.2 %all_gather.5 = bf16[2048,128]{1,0:T(8,128)(2,1)} all-gather(bf16[128,128]{1,0:T(8,128)(2,1)S(1)} %copy-done.11), channel_id=1, replica_groups=mesh['dp'=4,'head'=8,'ctx'=16] {'ctx'}, dimensions={0}, use_global_device_ids=true | all-gather | bytes 557056 | tf_op jit(solution)/shard_map/all_gather | solution.py:205
  113.2 14.2 %while.68 = (s32[]{:T(128)}, f32[6,128,128]{2,1,0:T(8,128)S(1)}, f32[6,128]{1,0:T(8,128)S(1)}, f32[6,128]{1,0:T(8,128)S(1)}, s32[2048]{0:T(1024)S(1)}, /*index=5...) while((s32[]{:T(128)}, f32[6,128,128]{2,1,0:T(8,128)S(1)}, ...), condition=%wide.region_3.4_spmd.clone, body=%wide.region_0.3_spmd.clone.sunk | while | flops 708284160 | bytes 6288607 | solution.py:32
  114.3 2.4 fusion.130
  117.9 2.4 fusion.130
  121.4 2.4 fusion.130
  125.0 2.4 fusion.130
  130.5 30.6 %while.69 = (s32[]{:T(128)}, f32[128,6,128]{0,2,1:T(8,128)}, f32[2048,256]{0,1:T(8,128)}, bf16[2048,128]{1,0:T(8,128)(2,1)S(1)}, s32[2048]{0:T(1024)S(1)}, /*ind...) while((s32[]{:T(128)}, f32[128,6,128]{0,2,1:T(8,128)}, ...), condition=%wide.region_5.6_spmd.clone, body=%wide.region_4.5_spmd.clone.sunk | while | flops 506888192 | bytes 12865837 | solution.py:32
  139.5 2.0 fusion.143
  147.4 2.0 fusion.143
  151.2 2.0 fusion.145
  155.3 2.0 fusion.143
  159.1 2.0 fusion.145
  162.4 14.2 %while.70 = (s32[]{:T(128)}, f32[6,128,128]{2,1,0:T(8,128)S(1)}, f32[6,128]{1,0:T(8,128)S(1)}, f32[6,128]{1,0:T(8,128)S(1)}, s32[2048]{0:T(1024)S(1)}, /*index=5...) while((s32[]{:T(128)}, f32[6,128,128]{2,1,0:T(8,128)S(1)}, ...), condition=%wide.region_9.10_spmd.clone, body=%wide.region_6.0_spmd.clone.sunk | while | flops 708284160 | bytes 6288607 | solution.py:32
  163.5 2.4 fusion.151
  167.1 2.4 fusion.151
  170.6 2.4 fusion.151
  174.2 2.4 fusion.151
  177.2 25.3 %while.71 = (s32[]{:T(128)}, f32[128,6,128]{0,2,1:T(8,128)}, f32[2048,256]{0,1:T(8,128)}, bf16[2048,128]{1,0:T(8,128)(2,1)S(1)}, s32[2048]{0:T(1024)S(1)}, /*ind...) while((s32[]{:T(128)}, f32[128,6,128]{0,2,1:T(8,128)}, ...), condition=%wide.region_11.12_spmd.clone, body=%wide.region_10.11_spmd.clone.sunk | while | flops 506888192 | bytes 16011621 | solution.py:32
  194.2 2.0 fusion.166
  200.5 2.0 fusion.166
  202.5 2.6 copy.55
  207.0 83.6 %reduce-scatter.2.cloned.1.call-done = bf16[128,256]{1,0:T(8,128)(2,1)} async-done(((bf16[2048,256]{1,0:T(8,128)(2,1)}), bf16[128,256]{1,0:T(8,128)(2,1)}) %reduce-scatter.2.cloned.1.call-update) | async-done | bytes 65552 | tf_op jit(solution)/shard_map/reduce_scatter | solution.py:212
  (228 shorter events, 59.1 us)
Async XLA Ops:
  7.2 49.7 %copy-start = (s32[2048]{0:T(1024)S(1)}, s32[2048]{0:T(1024)}, u32[]{:S(2)}) copy-start(s32[2048]{0:T(1024)} %param.17) | copy-start | bytes 24580
  7.2 283.4 %reduce-scatter.2.cloned.1.call-start = ((), (), s32[]{:S(2)}) async-start(), calls=%async_computation.1 | async-start | bytes 1114112 | tf_op jit(solution)/shard_map/reduce_scatter | solution.py:212
  56.8 11.9 %copy-start.9 = (bf16[128,768]{1,0:T(8,128)(2,1)S(1)}, bf16[128,768]{1,0:T(8,128)(2,1)}, u32[]{:S(2)}) copy-start(bf16[128,768]{1,0:T(8,128)(2,1)} %param.18) | copy-start | bytes 589828
  56.9 12.2 %copy-start.11 = (bf16[128,128]{1,0:T(8,128)(2,1)S(1)}, bf16[128,128]{1,0:T(8,128)(2,1)}, u32[]{:S(2)}) copy-start(bf16[128,128]{1,0:T(8,128)(2,1)} %param.21) | copy-start | bytes 98308
  135.4 2.0 copy-start.8
  143.3 2.0 copy-start.8
  151.2 2.1 copy-start.8
  159.1 2.0 copy-start.8
  162.4 14.2 %copy-start.10 = (bf16[128,768]{1,0:T(8,128)(2,1)S(1)}, bf16[128,768]{1,0:T(8,128)(2,1)}, u32[]{:S(2)}) copy-start(bf16[128,768]{1,0:T(8,128)(2,1)} %param.23) | copy-start | bytes 589828
  177.2 0.9 copy-start.5
  178.1 1.4 copy-start.1
  179.8 3.7 %copy-start.2 = (f32[128,6,128]{0,2,1:T(8,128)}, f32[128,6,128]{0,2,1:T(8,128)S(1)}, u32[]{:S(2)}) copy-start(f32[128,6,128]{0,2,1:T(8,128)S(1)} %fusion.164) | copy-start | bytes 1179652 | tf_op jit(solution)/shard_map/while
  181.5 2.0 copy-start.6
  184.4 1.4 copy-start.1
  186.1 3.7 %copy-start.2 = (f32[128,6,128]{0,2,1:T(8,128)}, f32[128,6,128]{0,2,1:T(8,128)S(1)}, u32[]{:S(2)}) copy-start(f32[128,6,128]{0,2,1:T(8,128)S(1)} %fusion.164) | copy-start | bytes 1179652 | tf_op jit(solution)/shard_map/while
  187.8 2.0 copy-start.6
  190.7 1.4 copy-start.1
  192.4 3.8 %copy-start.2 = (f32[128,6,128]{0,2,1:T(8,128)}, f32[128,6,128]{0,2,1:T(8,128)S(1)}, u32[]{:S(2)}) copy-start(f32[128,6,128]{0,2,1:T(8,128)S(1)} %fusion.164) | copy-start | bytes 1179652 | tf_op jit(solution)/shard_map/while
  194.2 2.1 copy-start.6
  197.0 1.4 copy-start.1
  198.8 3.8 %copy-start.2 = (f32[128,6,128]{0,2,1:T(8,128)}, f32[128,6,128]{0,2,1:T(8,128)S(1)}, u32[]{:S(2)}) copy-start(f32[128,6,128]{0,2,1:T(8,128)S(1)} %fusion.164) | copy-start | bytes 1179652 | tf_op jit(solution)/shard_map/while
  200.5 2.0 copy-start.6
  202.5 2.6 copy-start.4
  205.2 1.0 copy-start.3
  (7 other events, 5.9 us)
Sparse Core Ops, SparseCore 0:
  205.3 85.2 reduce-scatter.1
where the time goes:
time: 304 us; the launch traced here: 299 us
  blocking collectives  92.7 us (30%)
  waiting for transfers between devices  83.6 us (28%)
  matrix products  58.8 us (19%)
  local copies, waits for them, and re-layouts  25.2 us (8%)
  other arithmetic  23.1 us (8%)
  between operations  14.3 us (5%)
    reduce_scatter x1, waiting for transfers between devices, per_device(): lax.psum_scatter(key_terms.astype(jnp.bfloat16), 'ctx', scatter_dimension...  83.6 us
    all_gather x1, blocking collectives, per_device(): lax.all_gather(shared_keys, 'ctx', axis=0, tiled=True)  48.6 us
    all_gather x1, blocking collectives, per_device(): lax.all_gather(shared_values, 'ctx', axis=0, tiled=True)  44.2 us
    dot_general x8, matrix products, compute(): jnp.einsum('hrn,nd->hrd', weights, value_wide, precision=lax.Precision.HI...  19.4 us
    dynamic_update_slice x8, other arithmetic, compute(): lax.dynamic_update_slice_in_dim(key_terms, current + jnp.concatenate([key...  16.1 us
    gather x1, local copies, waits for them, and re-layouts, storage_layout(): return (positions, jnp.take(doc_ids, positions, axis=0))  11.8 us
    dot_general x8, matrix products, compute(): jnp.einsum('hrn,rhd->nd', score_grad, queries[layer_id], preferred_elemen...  10.5 us
    dot_general x8, matrix products, compute(): jnp.einsum('rhd,nd->hrn', cotangents[layer_id], value_block, preferred_el...  10.3 us
  transfers between devices with their start and end apart: 1, of which 1 were waited for; matrix products, arithmetic and copies ran while one was open for 1% of the time, Pallas kernels for 0%

commit v1 on v0

v1 whole, which is shorter than its diff:
```python
import functools
import math

import jax
import jax.numpy as jnp
from jax import lax
from jax.experimental import pallas as pl
from jax.experimental.pallas import tpu as pltpu
from jax.sharding import PartitionSpec as P

HD = 128
TILE = 256
COLS = 256
MASKED_SCORE = -1e30
NT = (((1,), (1,)), ((), ()))
NN = (((1,), (0,)), ((), ()))


def dot(left, right, dims):
    return lax.dot_general(left, right, dims, preferred_element_type=jnp.float32)


def attention_kernel(
    order_ref,
    doc_ref,
    q_first,
    q_second,
    g_first,
    g_second,
    kv_ref,
    dq_first,
    dq_second,
    kvg_ref,
    kv_sorted,
    q_rows,
    g_rows,
    scores_ref,
    grads_ref,
    key_sum,
    dq_sum,
):
    slabs = order_ref.shape[0]
    total = kv_ref.shape[0]
    slab = total // slabs
    own = q_first.shape[0] // slab
    heads = q_first.shape[1] // HD
    width = 2 * heads * slab
    first_slab = lax.axis_index("ctx") * own
    scale = 1.0 / math.sqrt(HD)
    scale2 = scale * math.log2(math.e)

    def to_sequence(i, carried):
        at = pl.multiple_of(order_ref[i] * slab, slab)
        kv_sorted[pl.ds(at, slab), :] = kv_ref[pl.ds(pl.multiple_of(i * slab, slab), slab), :]
        return carried

    lax.fori_loop(0, slabs, to_sequence, 0)
    kv_sorted[total:, :] = jnp.zeros((kv_sorted.shape[0] - total, 2 * HD), jnp.bfloat16)
    key_sum[...] = jnp.zeros_like(key_sum)

    for mine in range(own):
        rows = slice(mine * slab, (mine + 1) * slab)
        for layer, (q_ref, g_ref) in enumerate(((q_first, g_first), (q_second, g_second))):
            for head in range(heads):
                at = (layer * heads + head) * slab
                cols = slice(head * HD, (head + 1) * HD)
                q_rows[mine, at : at + slab, :] = q_ref[rows, cols]
                g_rows[mine, at : at + slab, :] = g_ref[rows, cols]

    docs = doc_ref[...]
    bounds = [jnp.sum((docs < d).astype(jnp.int32)) for d in (1, 2, 3)]

    def one_slab(mine, carried):
        pos0 = order_ref[first_slab + mine] * slab
        row_pos = pos0 + (lax.broadcasted_iota(jnp.int32, (1, HD), 1) & (slab - 1))
        row_doc = jnp.zeros((1, HD), jnp.int32)
        low = jnp.int32(0)
        for bound in bounds:
            row_doc = jnp.where(row_pos >= bound, bound, row_doc)
            low = jnp.where(pos0 >= bound, bound, low)
        low = (low // slab) * slab
        tiles = (pos0 + slab - low + (TILE - 1)) // TILE

        def forward(t, state):
            base = pl.multiple_of(low + t * TILE, slab)
            key_pos = base + lax.broadcasted_iota(jnp.int32, (TILE, HD), 0)
            allowed = (key_pos <= row_pos) & (key_pos >= row_doc)
            allowed = jnp.concatenate([allowed] * (COLS // HD), axis=1)
            keys = kv_sorted[pl.ds(base, TILE), :HD]
            values = kv_sorted[pl.ds(base, TILE), HD:]
            new = []
            for block, (top, norm, weighted) in enumerate(state):
                cols = slice(block * COLS, (block + 1) * COLS)
                s = dot(keys, q_rows[mine, cols, :], NT)
                s = jnp.where(allowed, s, MASKED_SCORE)
                scores_ref[t, :, cols] = s
                dp = dot(values, g_rows[mine, cols, :], NT)
                grads_ref[t, :, cols] = dp
                new_top = jnp.maximum(top, jnp.max(s, axis=0, keepdims=True))
                e = jnp.exp2((s - new_top) * scale2)
                fix = jnp.exp2((top - new_top) * scale2)
                norm = norm * fix + jnp.sum(e, axis=0, keepdims=True)
                weighted = weighted * fix + jnp.sum(e * dp, axis=0, keepdims=True)
                new.append((new_top, norm, weighted))
            return tuple(new)

        start = (
            jnp.full((1, COLS), MASKED_SCORE, jnp.float32),
            jnp.zeros((1, COLS), jnp.float32),
            jnp.zeros((1, COLS), jnp.float32),
        )
        state = lax.fori_loop(0, tiles, forward, (start,) * (width // COLS))
        stats = [
            (top * scale2 + jnp.log2(norm), weighted / norm) for (top, norm, weighted) in state
        ]
        dq_sum[...] = jnp.zeros_like(dq_sum)

        def backward(t, carried):
            base = pl.multiple_of(low + t * TILE, slab)
            keys_t = kv_sorted[pl.ds(base, TILE), :HD].T
            dk = jnp.zeros((TILE, HD), jnp.float32)
            dv = jnp.zeros((TILE, HD), jnp.float32)
            for block, (lse, delta) in enumerate(stats):
                cols = slice(block * COLS, (block + 1) * COLS)
                p = jnp.exp2(scores_ref[t, :, cols] * scale2 - lse)
                ds = (p * (grads_ref[t, :, cols] - delta)).astype(jnp.bfloat16)
                dv = dv + dot(p.astype(jnp.bfloat16), g_rows[mine, cols, :], NN)
                dk = dk + dot(ds, q_rows[mine, cols, :], NN)
                dq_sum[:, cols] += dot(keys_t, ds, NN)
            key_sum[pl.ds(base, TILE), :HD] += dk * scale
            key_sum[pl.ds(base, TILE), HD:] += dv
            return carried

        lax.fori_loop(0, tiles, backward, 0)
        dq = (dq_sum[...] * scale).T.astype(jnp.bfloat16)
        rows = pl.ds(pl.multiple_of(mine * slab, slab), slab)
        for layer, out in enumerate((dq_first, dq_second)):
            for head in range(heads):
                at = (layer * heads + head) * slab
                out[rows, head * HD : (head + 1) * HD] = dq[at : at + slab, :]
        return carried

    lax.fori_loop(0, own, one_slab, 0)

    def to_storage(i, carried):
        at = pl.multiple_of(order_ref[i] * slab, slab)
        to = pl.ds(pl.multiple_of(i * slab, slab), slab)
        kvg_ref[to, :] = key_sum[pl.ds(at, slab), :].astype(jnp.bfloat16)
        return carried

    lax.fori_loop(0, slabs, to_storage, 0)


def attention(slab_order, doc_ids, q_first, q_second, g_first, g_second, kv):
    rows, width = q_first.shape
    total = kv.shape[0]
    slab = total // slab_order.shape[0]
    own = rows // slab
    cols = 2 * (width // HD) * slab
    most = -(-(total // 2 + slab) // TILE)
    vmem = pl.BlockSpec(memory_space=pltpu.VMEM)
    return pl.pallas_call(
        attention_kernel,
        out_shape=(
            jax.ShapeDtypeStruct((rows, width), jnp.bfloat16),
            jax.ShapeDtypeStruct((rows, width), jnp.bfloat16),
            jax.ShapeDtypeStruct((total, 2 * HD), jnp.bfloat16),
        ),
        in_specs=[pl.BlockSpec(memory_space=pltpu.SMEM)] + [vmem] * 6,
        out_specs=(vmem,) * 3,
        scratch_shapes=[
            pltpu.VMEM((total + TILE, 2 * HD), jnp.bfloat16),
            pltpu.VMEM((own, cols, HD), jnp.bfloat16),
            pltpu.VMEM((own, cols, HD), jnp.bfloat16),
            pltpu.VMEM((most, TILE, cols), jnp.float32),
            pltpu.VMEM((most, TILE, cols), jnp.float32),
            pltpu.VMEM((total + TILE, 2 * HD), jnp.float32),
            pltpu.VMEM((HD, cols), jnp.float32),
        ],
        compiler_params=pltpu.CompilerParams(vmem_limit_bytes=40 * 1024 * 1024),
    )(slab_order, doc_ids.reshape(-1, HD), q_first, q_second, g_first, g_second, kv)


SIDE = 4
ALONG_X = [[x * SIDE + y for x in range(SIDE)] for y in range(SIDE)]
ALONG_Y = [[x * SIDE + y for y in range(SIDE)] for x in range(SIDE)]


def exchange(blocks, groups):
    return lax.all_to_all(blocks, "ctx", 0, 0, axis_index_groups=groups)


def spread(block, groups):
    copies = jnp.broadcast_to(block[None], (SIDE,) + block.shape)
    return exchange(copies, groups).reshape(SIDE * block.shape[0], block.shape[1])


def collect(terms, groups):
    parts = exchange(terms.reshape(SIDE, -1, terms.shape[1]), groups)
    return jnp.sum(parts.astype(jnp.float32), axis=0).astype(jnp.bfloat16)


def per_device(
    slab_order,
    doc_ids,
    query_first,
    query_second,
    shared_keys,
    shared_values,
    out_grad_first,
    out_grad_second,
):
    kv = jnp.concatenate([shared_keys, shared_values], axis=1)
    kv = spread(spread(kv, ALONG_Y), ALONG_X)
    dq_first, dq_second, terms = attention(
        slab_order, doc_ids, query_first, query_second, out_grad_first, out_grad_second, kv
    )
    summed = collect(collect(terms, ALONG_X), ALONG_Y)
    return (dq_first, dq_second, summed[:, :HD], summed[:, HD:])


def solution(mesh):
    rows = P(("dp", "ctx"), "head")
    return jax.shard_map(
        per_device,
        mesh=mesh,
        in_specs=(P("dp"), P("dp")) + (rows,) * 6,
        out_specs=(rows,) * 4,
        check_vma=False,
    )
```

time: 304 us -> 78.2 us (0.26); the launches traced: 299 us -> 77.8 us
  waiting for transfers between devices: 83.6 us -> 0 us
  matrix products: 58.8 us -> 0 us
  local copies, waits for them, and re-layouts: 25.2 us -> 1.37 us
  blocking collectives: 92.7 us -> 69.3 us
  other arithmetic: 23.1 us -> 1.08 us
  between operations: 14.3 us -> 0.71 us
  Pallas kernels: 0 us -> 5.38 us
    all_gather x2 -> x0, blocking collectives: 92.7 us -> none  [the longest x1 48.6 us: per_device(): lax.all_gather(shared_keys, 'ctx', axis=0, tiled=True)]
    reduce_scatter x1 -> x0, waiting for transfers between devices: 83.6 us -> none  [per_device(): lax.psum_scatter(key_terms.astype(jnp.bfloat16), 'ctx', scatter_dimension...]
    all_to_all x0 -> x4, blocking collectives: none -> 69.3 us  [exchange(): return lax.all_to_all(blocks, 'ctx', 0, 0, axis_index_groups=groups)]
    dot_general x56 -> x0, matrix products: 58.8 us -> none  [the longest x8 19.4 us: compute(): jnp.einsum('hrn,nd->hrd', weights, value_wide, precision=lax.Precision.HI...]
    dynamic_update_slice x8 -> x0, other arithmetic: 16.1 us -> none  [compute(): lax.dynamic_update_slice_in_dim(key_terms, current + jnp.concatenate([key...]
    gather x1 -> x0, local copies, waits for them, and re-layouts: 11.8 us -> none  [storage_layout(): return (positions, jnp.take(doc_ids, positions, axis=0))]
    pallas_call x0 -> x1, Pallas kernels: none -> 5.38 us  [attention(): pl.pallas_call(attention_kernel, out_shape=(jax.ShapeDtypeStruct((rows, w...]
    unnamed x22 -> x12, local copies, waits for them, and re-layouts: 4.95 us -> 0.66 us
  transfers between devices with their start and end apart: 1 -> 0, of which waited for: 1 -> 0; matrix products, arithmetic and copies ran while one was open for 1% -> 0% of each run, Pallas kernels for 0% -> 0%
where the time goes in v1:
time: 78.2 us; the launch traced here: 77.8 us
  blocking collectives  69.3 us (89%)
  Pallas kernels  5.38 us (7%)
  local copies, waits for them, and re-layouts  1.37 us (2%)
  other arithmetic  1.08 us (1%)
    all_to_all x4, blocking collectives, exchange(): return lax.all_to_all(blocks, 'ctx', 0, 0, axis_index_groups=groups)  69.3 us
    pallas_call x1, Pallas kernels, attention(): pl.pallas_call(attention_kernel, out_shape=(jax.ShapeDtypeStruct((rows, w...  5.38 us

profile of v1, /device:TPU:448, one launch (start us, length us, event | category | flops | bytes accessed | tf_op | source)
XLA Modules:
  0.0 77.8 jit_solution(13561941281790407578)
XLA Ops:
  0.6 0.8 %pad_maximum_fusion = bf16[128,256]{1,0:T(8,128)(2,1)S(1)} fusion(bf16[128,128]{1,0:T(8,128)(2,1)} %param.13, bf16[128,128]{1,0:T(8,128)(2,1)} %param.12), kind=kLoop, calls=%fused_computation | loop fusion | flops 131072 | bytes 131072 | tf_op jit(solution)/shard_map/concatenate | solution.py:213
  1.4 17.7 %all_to_all.20 = bf16[4,128,256]{2,1,0:T(8,128)(2,1)S(1)} all-to-all(bf16[4,128,256]{2,1,0:T(8,128)(2,1)S(1)} %broadcast_in_dim.6), channel_id=1, replica_groups={{0,1,2,3},{4,5,6,7},{8,9,10,11},{12,13,14,15},{16,17,18,19},{20,21,22,2..., dimensions={0} | all-to-all | bytes 524288 | tf_op jit(solution)/shard_map/all_to_all | solution.py:190
  19.2 0.1 broadcast_in_dim.15
  19.2 0.0 copy-start
  19.2 0.0 copy-start.1
  19.3 0.0 copy-start.2
  19.3 0.0 copy-start.3
  19.3 0.0 copy-start.4
  19.3 16.9 %all_to_all.21 = bf16[4,512,256]{2,1,0:T(8,128)(2,1)S(1)} all-to-all(bf16[4,512,256]{2,1,0:T(8,128)(2,1)S(1)} %broadcast_in_dim.15), channel_id=1, replica_groups={{0,4,8,12},{1,5,9,13},{2,6,10,14},{3,7,11,15},{16,20,24,28},{17,21,25,2..., dimensions={0} | all-to-all | bytes 2097152 | tf_op jit(solution)/shard_map/all_to_all | solution.py:190
  36.2 0.0 copy-start.5
  36.2 0.0 copy-done
  36.2 0.0 copy-done.1
  36.2 0.0 copy-done.2
  36.2 0.0 copy-done.3
  36.2 0.0 copy-done.4
  36.2 0.6 copy-done.5
  36.8 5.4 %shard_map.111 = (bf16[128,768]{1,0:T(8,128)(2,1)}, bf16[128,768]{1,0:T(8,128)(2,1)}, bf16[2048,256]{1,0:T(8,128)(2,1)S(1)}) custom-call(s32[32]{0:T(128)S(1)} %copy-done.5, s32[16,128]{1,0:T(8,128)S(1)} %bitcast.7, bf16[128,768]{1,0:T(8,128)(2,1)S(1)} %copy-done, bf16[128,768]{1,0:T(8,128)(2,1)S(1)} %copy-done.1, bf16[128,768]{1,0:T(8,128)(2,1)S(1)} %copy-done.2, ...), custom_call_target="tpu_custom_call" | custom-call | tf_op jit(solution)/shard_map/pallas_call | solution.py:162
  42.2 17.8 %all_to_all.22 = bf16[4,512,256]{2,1,0:T(8,128)(2,1)S(1)} all-to-all(bf16[4,512,256]{2,1,0:T(8,128)(2,1)S(1)} %bitcast.6), channel_id=1, replica_groups={{0,4,8,12},{1,5,9,13},{2,6,10,14},{3,7,11,15},{16,20,24,28},{17,21,25,2..., dimensions={0} | all-to-all | bytes 2097152 | tf_op jit(solution)/shard_map/all_to_all | solution.py:190
  60.1 0.3 reduce_sum.24
  60.3 16.9 %all_to_all.23 = bf16[4,128,256]{2,1,0:T(8,128)(2,1)S(1)} all-to-all(bf16[4,128,256]{2,1,0:T(8,128)(2,1)S(1)} %bitcast.9), channel_id=1, replica_groups={{0,1,2,3},{4,5,6,7},{8,9,10,11},{12,13,14,15},{16,17,18,19},{20,21,22,2..., dimensions={0} | all-to-all | bytes 524288 | tf_op jit(solution)/shard_map/all_to_all | solution.py:190
  77.2 0.6 fusion
  (2 shorter events, 0.1 us)
Async XLA Ops:
  19.2 17.0 %copy-start = (bf16[128,768]{1,0:T(8,128)(2,1)S(1)}, bf16[128,768]{1,0:T(8,128)(2,1)}, u32[]{:S(2)}) copy-start(bf16[128,768]{1,0:T(8,128)(2,1)} %q_first.1) | copy-start | bytes 589828
  19.2 16.9 %copy-start.1 = (bf16[128,768]{1,0:T(8,128)(2,1)S(1)}, bf16[128,768]{1,0:T(8,128)(2,1)}, u32[]{:S(2)}) copy-start(bf16[128,768]{1,0:T(8,128)(2,1)} %q_second.1) | copy-start | bytes 589828
  19.3 16.9 %copy-start.2 = (bf16[128,768]{1,0:T(8,128)(2,1)S(1)}, bf16[128,768]{1,0:T(8,128)(2,1)}, u32[]{:S(2)}) copy-start(bf16[128,768]{1,0:T(8,128)(2,1)} %g_first.1) | copy-start | bytes 589828
  19.3 16.9 %copy-start.3 = (bf16[128,768]{1,0:T(8,128)(2,1)S(1)}, bf16[128,768]{1,0:T(8,128)(2,1)}, u32[]{:S(2)}) copy-start(bf16[128,768]{1,0:T(8,128)(2,1)} %g_second.1) | copy-start | bytes 589828
  19.3 16.9 %copy-start.4 = (s32[2048]{0:T(1024)S(1)}, s32[2048]{0:T(1024)}, u32[]{:S(2)}) copy-start(s32[2048]{0:T(1024)} %param.9) | copy-start | bytes 24580
  36.2 0.7 copy-start.5

commit v2 on v1

--- a/solution.py
+++ b/solution.py
@@ -181,23 +181,8 @@
     )(slab_order, doc_ids.reshape(-1, HD), q_first, q_second, g_first, g_second, kv)
 
 
-SIDE = 4
-ALONG_X = [[x * SIDE + y for x in range(SIDE)] for y in range(SIDE)]
-ALONG_Y = [[x * SIDE + y for y in range(SIDE)] for x in range(SIDE)]
-
-
-def exchange(blocks, groups):
-    return lax.all_to_all(blocks, "ctx", 0, 0, axis_index_groups=groups)
-
-
-def spread(block, groups):
-    copies = jnp.broadcast_to(block[None], (SIDE,) + block.shape)
-    return exchange(copies, groups).reshape(SIDE * block.shape[0], block.shape[1])
-
-
-def collect(terms, groups):
-    parts = exchange(terms.reshape(SIDE, -1, terms.shape[1]), groups)
-    return jnp.sum(parts.astype(jnp.float32), axis=0).astype(jnp.bfloat16)
+def exchange(blocks):
+    return lax.all_to_all(blocks, "ctx", 0, 0)
 
 
 def per_device(
@@ -210,13 +195,16 @@
     out_grad_first,
     out_grad_second,
 ):
+    peers = lax.axis_size("ctx")
     kv = jnp.concatenate([shared_keys, shared_values], axis=1)
-    kv = spread(spread(kv, ALONG_Y), ALONG_X)
+    kv = exchange(jnp.broadcast_to(kv[None], (peers,) + kv.shape)).reshape(-1, 2 * HD)
     dq_first, dq_second, terms = attention(
         slab_order, doc_ids, query_first, query_second, out_grad_first, out_grad_second, kv
     )
-    summed = collect(collect(terms, ALONG_X), ALONG_Y)
-    return (dq_first, dq_second, summed[:, :HD], summed[:, HD:])
+    parts = exchange(terms.reshape(peers, -1, 2 * HD))
+    dk = jnp.sum(parts[:, :, :HD].astype(jnp.float32), axis=0).astype(jnp.bfloat16)
+    dv = jnp.sum(parts[:, :, HD:].astype(jnp.float32), axis=0).astype(jnp.bfloat16)
+    return (dq_first, dq_second, dk, dv)
 
 
 def solution(mesh):

time: 78.2 us -> 82.9 us (1.060)
  the two profiles are of different devices: /device:TPU:448 before, /device:TPU:384 now
where the time goes in v2:
time: 82.9 us; the launch traced here: 82.6 us
  blocking collectives  75.2 us (91%)
  Pallas kernels  4.43 us (5%)
  other arithmetic  1.55 us (2%)
    all_to_all x2, blocking collectives, exchange(): return lax.all_to_all(blocks, 'ctx', 0, 0)  75.2 us
    pallas_call x1, Pallas kernels, attention(): pl.pallas_call(attention_kernel, out_shape=(jax.ShapeDtypeStruct((rows, w...  4.43 us

profile of v2, /device:TPU:384, one launch (start us, length us, event | category | flops | bytes accessed | tf_op | source)
XLA Modules:
  0.0 82.6 jit_solution(17776779436242956650)
XLA Ops:
  0.6 0.8 pad_maximum_fusion
  1.4 0.1 broadcast_in_dim.2
  1.5 0.0 copy-start
  1.5 0.0 copy-start.1
  1.5 0.0 copy-start.2
  1.6 0.0 copy-start.3
  1.6 0.0 copy-start.4
  1.6 39.6 %all_to_all.10 = bf16[16,128,256]{2,1,0:T(8,128)(2,1)S(1)} all-to-all(bf16[16,128,256]{2,1,0:T(8,128)(2,1)S(1)} %broadcast_in_dim.2), channel_id=1, replica_groups=mesh['dp'=4,'head'=8,'ctx'=16] {'ctx'}, dimensions={0} | all-to-all | bytes 2097152 | tf_op jit(solution)/shard_map/all_to_all | solution.py:185
  41.2 0.0 copy-start.5
  41.2 0.0 copy-done
  41.2 0.0 copy-done.1
  41.2 0.0 copy-done.2
  41.2 0.0 copy-done.3
  41.2 0.0 copy-done.4
  41.3 0.6 copy-done.5
  41.9 4.4 %shard_map.111 = (bf16[128,768]{1,0:T(8,128)(2,1)}, bf16[128,768]{1,0:T(8,128)(2,1)}, bf16[2048,256]{1,0:T(8,128)(2,1)S(1)}) custom-call(s32[32]{0:T(128)S(1)} %copy-done.5, s32[16,128]{1,0:T(8,128)S(1)} %bitcast.5, bf16[128,768]{1,0:T(8,128)(2,1)S(1)} %copy-done, bf16[128,768]{1,0:T(8,128)(2,1)S(1)} %copy-done.1, bf16[128,768]{1,0:T(8,128)(2,1)S(1)} %copy-done.2, ...), custom_call_target="tpu_custom_call" | custom-call | tf_op jit(solution)/shard_map/pallas_call | solution.py:162
  46.3 35.5 %all_to_all.11 = bf16[16,128,256]{2,1,0:T(8,128)(2,1)S(1)} all-to-all(bf16[16,128,256]{2,1,0:T(8,128)(2,1)S(1)} %bitcast.4), channel_id=1, replica_groups=mesh['dp'=4,'head'=8,'ctx'=16] {'ctx'}, dimensions={0} | all-to-all | bytes 2097152 | tf_op jit(solution)/shard_map/all_to_all | solution.py:185
  81.8 0.8 slice_reduce_fusion
Async XLA Ops:
  1.5 39.7 %copy-start = (bf16[128,768]{1,0:T(8,128)(2,1)S(1)}, bf16[128,768]{1,0:T(8,128)(2,1)}, u32[]{:S(2)}) copy-start(bf16[128,768]{1,0:T(8,128)(2,1)} %q_first.1) | copy-start | bytes 589828
  1.5 39.7 %copy-start.1 = (bf16[128,768]{1,0:T(8,128)(2,1)S(1)}, bf16[128,768]{1,0:T(8,128)(2,1)}, u32[]{:S(2)}) copy-start(bf16[128,768]{1,0:T(8,128)(2,1)} %q_second.1) | copy-start | bytes 589828
  1.5 39.7 %copy-start.2 = (bf16[128,768]{1,0:T(8,128)(2,1)S(1)}, bf16[128,768]{1,0:T(8,128)(2,1)}, u32[]{:S(2)}) copy-start(bf16[128,768]{1,0:T(8,128)(2,1)} %g_first.1) | copy-start | bytes 589828
  1.6 39.7 %copy-start.3 = (bf16[128,768]{1,0:T(8,128)(2,1)S(1)}, bf16[128,768]{1,0:T(8,128)(2,1)}, u32[]{:S(2)}) copy-start(bf16[128,768]{1,0:T(8,128)(2,1)} %g_second.1) | copy-start | bytes 589828
  1.6 39.7 %copy-start.4 = (s32[2048]{0:T(1024)S(1)}, s32[2048]{0:T(1024)}, u32[]{:S(2)}) copy-start(s32[2048]{0:T(1024)} %param.9) | copy-start | bytes 24580
  41.2 0.7 copy-start.5

commit v3 on v1

v3 whole, which is shorter than its diff:
```python
import functools
import math

import jax
import jax.numpy as jnp
from jax import lax
from jax.experimental import pallas as pl
from jax.experimental.pallas import tpu as pltpu
from jax.sharding import PartitionSpec as P

HD = 128
SIZES = (256, 512, 768, 1024, 1152)
CHUNK = 512
FACTS = 48
MASKED_SCORE = -1e30
NT = (((1,), (1,)), ((), ()))
NN = (((1,), (0,)), ((), ()))


def dot(left, right, dims):
    return lax.dot_general(left, right, dims, preferred_element_type=jnp.float32)


def prepare_kernel(
    order_ref, doc_ref, q_first, q_second, g_first, g_second, q_rows, g_rows, facts
):
    slabs = order_ref.shape[0]
    own = q_rows.shape[0]
    slab = q_first.shape[0] // own
    heads = q_first.shape[1] // HD
    first_slab = lax.axis_index("ctx") * own
    for i in range(slabs, FACTS):
        facts[i] = 0

    def invert(i, carried):
        facts[order_ref[i]] = i
        return carried

    lax.fori_loop(0, slabs, invert, 0)
    docs = doc_ref[...]
    for i in range(3):
        facts[FACTS + i] = jnp.sum((docs <= i).astype(jnp.int32))
    for mine in range(own):
        facts[FACTS + 3 + mine] = order_ref[first_slab + mine]
        rows = slice(mine * slab, (mine + 1) * slab)
        for layer, (q_ref, g_ref) in enumerate(((q_first, g_first), (q_second, g_second))):
            for head in range(heads):
                at = (layer * heads + head) * slab
                cols = slice(head * HD, (head + 1) * HD)
                q_rows[mine, at : at + slab, :] = q_ref[rows, cols]
                g_rows[mine, at : at + slab, :] = g_ref[rows, cols]


def key_range(facts, mine, slab):
    pos0 = facts[FACTS + 3 + mine] * slab
    low = jnp.int32(0)
    for i in range(3):
        low = jnp.where(pos0 >= facts[FACTS + i], facts[FACTS + i], low)
    low = low // slab
    return pos0, low, pos0 + slab - low * slab


def for_size(need, work):
    for i, size in enumerate(SIZES):
        fits = need <= size
        if i:
            fits = fits & (need > SIZES[i - 1])
        pl.when(fits)(functools.partial(work, size))


def places(facts, low, start, size, slab):
    first = low + start // slab
    return [
        pl.ds(pl.multiple_of(facts[first + j] * slab, slab), slab) for j in range(size // slab)
    ]


def chunks(size):
    return [(start, min(CHUNK, size - start)) for start in range(0, size, CHUNK)]


def main_kernel(
    slab, facts, kv_ref, q_rows, g_rows, ds_ref, kvg_ref, scores_ref, grads_ref, key_sum
):
    own, width, _ = q_rows.shape
    scale = 1.0 / math.sqrt(HD)
    scale2 = scale * math.log2(math.e)
    key_sum[...] = jnp.zeros_like(key_sum)

    def one_slab(mine, carried):
        pos0, low, need = key_range(facts, mine, slab)
        row_pos = pos0 + (lax.broadcasted_iota(jnp.int32, (1, HD), 1) & (slab - 1))
        row_doc = jnp.zeros((1, HD), jnp.int32)
        for i in range(3):
            row_doc = jnp.where(row_pos >= facts[FACTS + i], facts[FACTS + i], row_doc)

        def work(size):
            q, g = q_rows[mine], g_rows[mine]
            top = jnp.full((1, width), MASKED_SCORE, jnp.float32)
            norm = weighted = jnp.zeros((1, width), jnp.float32)
            for start, part in chunks(size):
                key_pos = low * slab + start + lax.broadcasted_iota(jnp.int32, (part, HD), 0)
                allowed = (key_pos <= row_pos) & (key_pos >= row_doc)
                allowed = jnp.concatenate([allowed] * (width // HD), axis=1)
                at = places(facts, low, start, part, slab)
                rows = slice(start, start + part)
                keys = jnp.concatenate([kv_ref[a, :HD] for a in at], axis=0)
                values = jnp.concatenate([kv_ref[a, HD:] for a in at], axis=0)
                s = jnp.where(allowed, dot(keys, q, NT) * scale2, MASKED_SCORE)
                scores_ref[rows, :] = s
                dp = dot(values, g, NT)
                grads_ref[rows, :] = dp
                new_top = jnp.maximum(top, jnp.max(s, axis=0, keepdims=True))
                e = jnp.exp2(s - new_top)
                fix = jnp.exp2(top - new_top)
                norm = norm * fix + jnp.sum(e, axis=0, keepdims=True)
                weighted = weighted * fix + jnp.sum(e * dp, axis=0, keepdims=True)
                top = new_top
            lse = top + jnp.log2(norm)
            delta = weighted / norm
            for start, part in chunks(size):
                at = places(facts, low, start, part, slab)
                rows = slice(start, start + part)
                p = jnp.exp2(scores_ref[rows, :] - lse)
                ds = (p * (grads_ref[rows, :] - delta)).astype(jnp.bfloat16)
                ds_ref[mine, rows, :] = ds
                dv = dot(p.astype(jnp.bfloat16), g, NN)
                dk = dot(ds, q, NN)
                for j, a in enumerate(at):
                    piece = slice(j * slab, (j + 1) * slab)
                    key_sum[a, :HD] += dk[piece] * scale
                    key_sum[a, HD:] += dv[piece]

        for_size(need, work)
        return carried

    lax.fori_loop(0, own, one_slab, 0)
    kvg_ref[...] = key_sum[...].astype(jnp.bfloat16)


def query_kernel(facts, kv_ref, ds_ref, dq_first, dq_second):
    own = ds_ref.shape[0]
    slab = dq_first.shape[0] // own
    heads = dq_first.shape[1] // HD
    scale = 1.0 / math.sqrt(HD)

    def one_slab(mine, carried):
        _, low, need = key_range(facts, mine, slab)
        rows = pl.ds(pl.multiple_of(mine * slab, slab), slab)

        def work(size):
            at = places(facts, low, 0, size, slab)
            keys = jnp.concatenate([kv_ref[a, :HD] for a in at], axis=0)
            dq = dot(keys.T, ds_ref[mine, :size, :], NN) * scale
            dq = dq.T.astype(jnp.bfloat16)
            for layer, out in enumerate((dq_first, dq_second)):
                for head in range(heads):
                    at = (layer * heads + head) * slab
                    out[rows, head * HD : (head + 1) * HD] = dq[at : at + slab, :]

        for_size(need, work)
        return carried

    lax.fori_loop(0, own, one_slab, 0)


def cost(flops, size):
    return pl.CostEstimate(flops=flops, bytes_accessed=size, transcendentals=0)


VMEM = pl.BlockSpec(memory_space=pltpu.VMEM)
SMEM = pl.BlockSpec(memory_space=pltpu.SMEM)
ROOM = pltpu.CompilerParams(vmem_limit_bytes=40 * 1024 * 1024)


def prepare(slab_order, doc_ids, q_first, q_second, g_first, g_second, own):
    rows, width = q_first.shape
    stacked = jax.ShapeDtypeStruct((own, 2 * rows * (width // HD) // own, HD), jnp.bfloat16)
    return pl.pallas_call(
        prepare_kernel,
        out_shape=(stacked, stacked, jax.ShapeDtypeStruct((FACTS + 8,), jnp.int32)),
        in_specs=[SMEM] + [VMEM] * 5,
        out_specs=(VMEM, VMEM, SMEM),
        cost_estimate=cost(0, 16 * rows * width),
    )(slab_order, doc_ids.reshape(-1, HD), q_first, q_second, g_first, g_second)


def key_terms(facts, kv, q_rows, g_rows, slab):
    own, cols, _ = q_rows.shape
    most = SIZES[-1]
    return pl.pallas_call(
        functools.partial(main_kernel, slab),
        out_shape=(
            jax.ShapeDtypeStruct((own, most, cols), jnp.bfloat16),
            jax.ShapeDtypeStruct(kv.shape, jnp.bfloat16),
        ),
        in_specs=[SMEM] + [VMEM] * 3,
        out_specs=(VMEM,) * 2,
        scratch_shapes=[
            pltpu.VMEM((most, cols), jnp.float32),
            pltpu.VMEM((most, cols), jnp.float32),
            pltpu.VMEM(kv.shape, jnp.float32),
        ],
        compiler_params=ROOM,
        cost_estimate=cost(8 * own * most * cols * HD, 4 * own * most * cols),
    )(facts, kv, q_rows, g_rows)


def query_grads(facts, kv, ds, rows, width):
    out = jax.ShapeDtypeStruct((rows, width), jnp.bfloat16)
    return pl.pallas_call(
        query_kernel,
        out_shape=(out, out),
        in_specs=[SMEM] + [VMEM] * 2,
        out_specs=(VMEM,) * 2,
        compiler_params=ROOM,
        cost_estimate=cost(2 * ds.size * HD, 2 * ds.size),
    )(facts, kv, ds)


SIDE = 4
ALONG_X = [[x * SIDE + y for x in range(SIDE)] for y in range(SIDE)]
ALONG_Y = [[x * SIDE + y for y in range(SIDE)] for x in range(SIDE)]


def exchange(blocks, groups):
    return lax.all_to_all(blocks, "ctx", 0, 0, axis_index_groups=groups)


def spread(block, groups):
    copies = jnp.broadcast_to(block[None], (SIDE,) + block.shape)
    return exchange(copies, groups).reshape(SIDE * block.shape[0], block.shape[1])


def per_device(
    slab_order,
    doc_ids,
    query_first,
    query_second,
    shared_keys,
    shared_values,
    out_grad_first,
    out_grad_second,
):
    rows, width = query_first.shape
    slab = rows * lax.axis_size("ctx") // slab_order.shape[0]
    own = rows // slab
    kv = jnp.concatenate([shared_keys, shared_values], axis=1)
    kv = spread(spread(kv, ALONG_Y), ALONG_X)
    q_rows, g_rows, facts = prepare(
        slab_order, doc_ids, query_first, query_second, out_grad_first, out_grad_second, own
    )
    ds, terms = key_terms(facts, kv, q_rows, g_rows, slab)
    dq_first, dq_second = query_grads(facts, kv, ds, rows, width)
    parts = exchange(terms.reshape(SIDE, -1, 2 * HD), ALONG_X)
    summed = jnp.sum(parts.astype(jnp.float32), axis=0).astype(jnp.bfloat16)
    parts = exchange(summed.reshape(SIDE, -1, 2 * HD), ALONG_Y)
    dk = jnp.sum(parts[:, :, :HD].astype(jnp.float32), axis=0).astype(jnp.bfloat16)
    dv = jnp.sum(parts[:, :, HD:].astype(jnp.float32), axis=0).astype(jnp.bfloat16)
    return (dq_first, dq_second, dk, dv)


def solution(mesh):
    rows = P(("dp", "ctx"), "head")
    return jax.shard_map(
        per_device,
        mesh=mesh,
        in_specs=(P("dp"), P("dp")) + (rows,) * 6,
        out_specs=(rows,) * 4,
        check_vma=False,
    )
```

time: 78.2 us -> 79.8 us (1.020)
  blocking collectives: 69.3 us -> 32.3 us
  waiting for transfers between devices: 0 us -> 15.5 us
  starting transfers between devices: 0 us -> 13.2 us
  local copies, waits for them, and re-layouts: 1.37 us -> 7.45 us
  Pallas kernels: 5.38 us -> 7.71 us
  other arithmetic: 1.08 us -> 2.35 us
    all_to_all x4 -> x2, blocking collectives: 69.3 us -> 32.3 us  [exchange(): return lax.all_to_all(blocks, 'ctx', 0, 0, axis_index_groups=groups)]
    all_to_all x0 -> x2, waiting for transfers between devices: none -> 15.5 us  [exchange(): return lax.all_to_all(blocks, 'ctx', 0, 0, axis_index_groups=groups)]
    all_to_all x0 -> x2, starting transfers between devices: none -> 13.2 us  [exchange(): return lax.all_to_all(blocks, 'ctx', 0, 0, axis_index_groups=groups)]
    unnamed x12, local copies, waits for them, and re-layouts: 0.66 us -> 6.39 us
    pallas_call x1 -> x3, Pallas kernels: 5.38 us -> 7.71 us  [the longest x1 3.1 us: key_terms(): pl.pallas_call(functools.partial(main_kernel, slab), out_shape=(jax.Shape...]
    reduce_sum x2, other arithmetic: 0.3 us -> 1.56 us  [the longest x1 0.9 us: per_device(): summed = jnp.sum(parts.astype(jnp.float32), axis=0).astype(jnp.bfloat16)]
    broadcast_in_dim x2, local copies, waits for them, and re-layouts: 0.09 us -> 1.06 us  [spread(): copies = jnp.broadcast_to(block[None], (SIDE,) + block.shape)]
  transfers between devices with their start and end apart: 0 -> 2, of which waited for: 0 -> 2; matrix products, arithmetic and copies ran while one was open for 0% -> 0% of each run, Pallas kernels for 0% -> 6%
where the time goes in v3:
time: 79.8 us; the launch traced here: 79.2 us
  blocking collectives  32.3 us (40%)
  waiting for transfers between devices  15.5 us (19%)
  starting transfers between devices  13.2 us (17%)
  Pallas kernels  7.71 us (10%)
  local copies, waits for them, and re-layouts  7.45 us (9%)
  other arithmetic  2.35 us (3%)
    all_to_all x2, blocking collectives, exchange(): return lax.all_to_all(blocks, 'ctx', 0, 0, axis_index_groups=groups)  32.3 us
    all_to_all x2, waiting for transfers between devices, exchange(): return lax.all_to_all(blocks, 'ctx', 0, 0, axis_index_groups=groups)  15.5 us
    all_to_all x2, starting transfers between devices, exchange(): return lax.all_to_all(blocks, 'ctx', 0, 0, axis_index_groups=groups)  13.2 us
    unnamed x12, local copies, waits for them, and re-layouts  6.39 us
    pallas_call x1, Pallas kernels, key_terms(): pl.pallas_call(functools.partial(main_kernel, slab), out_shape=(jax.Shape...  3.1 us
    pallas_call x1, Pallas kernels, prepare(): pl.pallas_call(prepare_kernel, out_shape=(stacked, stacked, jax.ShapeDtyp...  2.55 us
    pallas_call x1, Pallas kernels, query_grads(): pl.pallas_call(query_kernel, out_shape=(out, out), in_specs=[SMEM] + [VME...  2.07 us
  transfers between devices with their start and end apart: 2, of which 2 were waited for; matrix products, arithmetic and copies ran while one was open for 0% of the time, Pallas kernels for 6%

profile of v3, /device:TPU:448, one launch (start us, length us, event | category | flops | bytes accessed | tf_op | source)
XLA Modules:
  0.0 79.2 jit_solution(11846133170054029250)
XLA Ops:
  0.6 0.8 pad_maximum_fusion
  1.4 17.7 %all_to_all.20 = bf16[4,128,256]{2,1,0:T(8,128)(2,1)S(1)} all-to-all(bf16[4,128,256]{2,1,0:T(8,128)(2,1)S(1)} %broadcast_in_dim.6), channel_id=1, replica_groups={{0,1,2,3},{4,5,6,7},{8,9,10,11},{12,13,14,15},{16,17,18,19},{20,21,22,2..., dimensions={0} | all-to-all | bytes 524288 | tf_op jit(solution)/shard_map/all_to_all | solution.py:227
  19.2 1.0 %broadcast_in_dim.15 = bf16[4,512,256]{2,1,0:T(8,128)(2,1)} broadcast(bf16[512,256]{1,0:T(8,128)(2,1)S(1)} %bitcast.8), dimensions={1,2} | broadcast | bytes 1310720 | tf_op jit(solution)/shard_map/broadcast_in_dim | solution.py:231
  20.2 4.3 %all-to-all-start.1 = ((bf16[4,512,256]{2,1,0:T(8,128)(2,1)}), bf16[4,512,256]{2,1,0:T(8,128)(2,1)S(1)}, u32[]{:S(2)}, u32[]{:S(2)}) async-start(bf16[4,512,256]{2,1,0:T(8,128)(2,1)} %broadcast_in_dim.15), calls=%async_computation.1 | async-start | bytes 2097152 | tf_op jit(solution)/shard_map/all_to_all | solution.py:227
  24.5 2.5 %shard_map.111 = (bf16[2,768,128]{2,1,0:T(8,128)(2,1)}, bf16[2,768,128]{2,1,0:T(8,128)(2,1)}, s32[56]{0:T(128)}) custom-call(s32[32]{0:T(128)} %order_ref.1, s32[16,128]{1,0:T(8,128)} %bitcast.9, bf16[128,768]{1,0:T(8,128)(2,1)} %q_first.1, bf16[128,768]{1,0:T(8,128)(2,1)} %q_second.1, bf16[128,768]{1,0:T(8,128)(2,1)} %g_first.1, bf16[128,768]{1,0:T(8,128)(2,1)} %g_second.1), custom_call_target="tpu_custom_call" | custom-call | bytes 1572864 | tf_op jit(solution)/shard_map/pallas_call | solution.py:179
  27.0 10.1 %all-to-all-done.1 = bf16[4,512,256]{2,1,0:T(8,128)(2,1)S(1)} async-done(((bf16[4,512,256]{2,1,0:T(8,128)(2,1)}), bf16[4,512,256]{2,1,0:T(8,128)(2,1)S(1)}, u32[]{:S(2)}, u32[]{:S(2)}) %all-to-all-start.1) | async-done | bytes 1048608 | tf_op jit(solution)/shard_map/all_to_all | solution.py:227
  37.2 0.0 copy-start.2
  37.2 0.7 copy-done.2
  37.8 0.0 copy-start.4
  37.8 1.0 %copy-done.4 = bf16[2,768,128]{2,1,0:T(8,128)(2,1)S(1)} copy-done((bf16[2,768,128]{2,1,0:T(8,128)(2,1)S(1)}, bf16[2,768,128]{2,1,0:T(8,128)(2,1)}, u32[]{:S(2)}) %copy-start.4) | copy-done | bytes 393240
  38.8 0.0 copy-start.5
  38.8 1.0 %copy-done.5 = bf16[2,768,128]{2,1,0:T(8,128)(2,1)S(1)} copy-done((bf16[2,768,128]{2,1,0:T(8,128)(2,1)S(1)}, bf16[2,768,128]{2,1,0:T(8,128)(2,1)}, u32[]{:S(2)}) %copy-start.5) | copy-done | bytes 393240
  39.8 3.1 %shard_map.112 = (bf16[2,1152,768]{2,1,0:T(8,128)(2,1)S(1)}, bf16[2048,256]{1,0:T(8,128)(2,1)S(1)}) custom-call(s32[56]{0:T(128)S(1)} %copy-done.2, bf16[2048,256]{1,0:T(8,128)(2,1)S(1)} %bitcast.5, bf16[2,768,128]{2,1,0:T(8,128)(2,1)S(1)} %copy-done.4, bf16[2,768,128]{2,1,0:T(8,128)(2,1)S(1)} %copy-done.5), custom_call_target="tpu_custom_call" | custom-call | flops 1811939328 | bytes 7077888 | tf_op jit(solution)/shard_map/pallas_call | solution.py:191
  42.9 0.0 copy-start
  42.9 1.7 %copy-done = bf16[2,1152,768]{2,1,0:T(8,128)(2,1)} copy-done((bf16[2,1152,768]{2,1,0:T(8,128)(2,1)}, bf16[2,1152,768]{2,1,0:T(8,128)(2,1)S(1)}, u32[]{:S(2)}) %copy-start) | copy-done | bytes 3538968
  44.7 0.0 copy-start.3
  44.7 14.6 %all_to_all.21 = bf16[4,512,256]{2,1,0:T(8,128)(2,1)S(1)} all-to-all(bf16[4,512,256]{2,1,0:T(8,128)(2,1)S(1)} %bitcast.7), channel_id=1, replica_groups={{0,4,8,12},{1,5,9,13},{2,6,10,14},{3,7,11,15},{16,20,24,28},{17,21,25,2..., dimensions={0} | all-to-all | bytes 2097152 | tf_op jit(solution)/shard_map/all_to_all | solution.py:227
  59.3 0.9 %reduce_sum.36 = bf16[512,256]{1,0:T(8,128)(2,1)} reduce(bf16[4,512,256]{2,1,0:T(8,128)(2,1)S(1)} %all_to_all.21, bf16[]{:T(256)} %constant.4.clone.1), dimensions={0}, to_apply=%region_0.0 | reduce | flops 393216 | bytes 1310722 | tf_op jit(solution)/shard_map/reduce_sum | solution.py:256
  60.2 8.9 %all-to-all-start.3 = ((bf16[4,128,256]{2,1,0:T(8,128)(2,1)}), bf16[4,128,256]{2,1,0:T(8,128)(2,1)S(1)}, u32[]{:S(2)}, u32[]{:S(2)}) async-start(bf16[4,128,256]{2,1,0:T(8,128)(2,1)} %bitcast.4), calls=%async_computation.3 | async-start | bytes 524288 | tf_op jit(solution)/shard_map/all_to_all | solution.py:227
  69.1 0.0 copy-done.3
  69.1 2.0 %copy-done.1 = bf16[2,1152,768]{2,1,0:T(8,128)(2,1)S(1)} copy-done((bf16[2,1152,768]{2,1,0:T(8,128)(2,1)S(1)}, bf16[2,1152,768]{2,1,0:T(8,128)(2,1)}, u32[]{:S(2)}) %copy-start.1) | copy-done | bytes 3538968
  71.1 2.1 %shard_map.113 = (bf16[128,768]{1,0:T(8,128)(2,1)}, bf16[128,768]{1,0:T(8,128)(2,1)}) custom-call(s32[56]{0:T(128)S(1)} %copy-done.3, bf16[2048,256]{1,0:T(8,128)(2,1)S(1)} %bitcast.6, bf16[2,1152,768]{2,1,0:T(8,128)(2,1)S(1)} %copy-done.1), custom_call_target="tpu_custom_call" | custom-call | flops 452984832 | bytes 3538944 | tf_op jit(solution)/shard_map/pallas_call | solution.py:211
  73.1 5.4 %all-to-all-done.3 = bf16[4,128,256]{2,1,0:T(8,128)(2,1)S(1)} async-done(((bf16[4,128,256]{2,1,0:T(8,128)(2,1)}), bf16[4,128,256]{2,1,0:T(8,128)(2,1)S(1)}, u32[]{:S(2)}, u32[]{:S(2)}) %all-to-all-start.3) | async-done | bytes 262176 | tf_op jit(solution)/shard_map/all_to_all | solution.py:227
  78.6 0.7 slice_reduce_fusion
  (2 shorter events, 0.0 us)
Async XLA Ops:
  20.2 17.0 %all-to-all-start.1 = ((bf16[4,512,256]{2,1,0:T(8,128)(2,1)}), bf16[4,512,256]{2,1,0:T(8,128)(2,1)S(1)}, u32[]{:S(2)}, u32[]{:S(2)}) async-start(bf16[4,512,256]{2,1,0:T(8,128)(2,1)} %broadcast_in_dim.15), calls=%async_computation.1 | async-start | bytes 2097152 | tf_op jit(solution)/shard_map/all_to_all | solution.py:227
  37.2 0.7 copy-start.2
  37.8 1.0 %copy-start.4 = (bf16[2,768,128]{2,1,0:T(8,128)(2,1)S(1)}, bf16[2,768,128]{2,1,0:T(8,128)(2,1)}, u32[]{:S(2)}) copy-start(bf16[2,768,128]{2,1,0:T(8,128)(2,1)} %get-tuple-element.12.q_rows) | copy-start | bytes 1179652
  38.8 1.0 %copy-start.5 = (bf16[2,768,128]{2,1,0:T(8,128)(2,1)S(1)}, bf16[2,768,128]{2,1,0:T(8,128)(2,1)}, u32[]{:S(2)}) copy-start(bf16[2,768,128]{2,1,0:T(8,128)(2,1)} %get-tuple-element.13.g_rows) | copy-start | bytes 1179652
  42.9 1.7 %copy-start = (bf16[2,1152,768]{2,1,0:T(8,128)(2,1)}, bf16[2,1152,768]{2,1,0:T(8,128)(2,1)S(1)}, u32[]{:S(2)}) copy-start(bf16[2,1152,768]{2,1,0:T(8,128)(2,1)S(1)} %get-tuple-element.14.ds_ref) | copy-start | bytes 10616836
  44.7 24.4 %copy-start.3 = (s32[56]{0:T(128)S(1)}, s32[56]{0:T(128)}, u32[]{:S(2)}) copy-start(s32[56]{0:T(128)} %get-tuple-element.11.facts) | copy-start | bytes 676
  60.2 18.4 %all-to-all-start.3 = ((bf16[4,128,256]{2,1,0:T(8,128)(2,1)}), bf16[4,128,256]{2,1,0:T(8,128)(2,1)S(1)}, u32[]{:S(2)}, u32[]{:S(2)}) async-start(bf16[4,128,256]{2,1,0:T(8,128)(2,1)} %bitcast.4), calls=%async_computation.3 | async-start | bytes 524288 | tf_op jit(solution)/shard_map/all_to_all | solution.py:227
  69.1 2.0 %copy-start.1 = (bf16[2,1152,768]{2,1,0:T(8,128)(2,1)S(1)}, bf16[2,1152,768]{2,1,0:T(8,128)(2,1)}, u32[]{:S(2)}) copy-start(bf16[2,1152,768]{2,1,0:T(8,128)(2,1)} %copy-done) | copy-start | bytes 10616836

commit v4 on v3

v4 whole, which is shorter than its diff:
```python
import functools
import math

import jax
import jax.numpy as jnp
from jax import lax
from jax.experimental import pallas as pl
from jax.experimental.pallas import tpu as pltpu
from jax.sharding import PartitionSpec as P

HD = 128
SIZES = (256, 512, 768, 1024, 1152)
CHUNK = 512
PLACES = 56
MASKED_SCORE = -1e30
NT = (((1,), (1,)), ((), ()))
NN = (((1,), (0,)), ((), ()))


def dot(left, right, dims):
    return lax.dot_general(left, right, dims, preferred_element_type=jnp.float32)


def for_size(need, work):
    for i, size in enumerate(SIZES):
        fits = need <= size
        if i:
            fits = fits & (need > SIZES[i - 1])
        pl.when(fits)(functools.partial(work, size))


def places(facts, low, start, size, slab):
    first = low + start // slab
    return [
        pl.ds(pl.multiple_of(facts[first + j] * slab, slab), slab) for j in range(size // slab)
    ]


def chunks(size):
    return [(start, min(CHUNK, size - start)) for start in range(0, size, CHUNK)]


def attention_kernel(
    order_hbm,
    doc_ref,
    q_first,
    q_second,
    g_first,
    g_second,
    kv_ref,
    dq_first,
    dq_second,
    kvg_ref,
    order_ref,
    facts,
    q_rows,
    g_rows,
    scores_ref,
    grads_ref,
    ds_ref,
    key_sum,
    order_sem,
):
    slabs = order_ref.shape[0]
    own, width, _ = q_rows.shape
    slab = q_first.shape[0] // own
    heads = q_first.shape[1] // HD
    scale = 1.0 / math.sqrt(HD)
    scale2 = scale * math.log2(math.e)
    order_copy = pltpu.make_async_copy(order_hbm, order_ref, order_sem)
    order_copy.start()

    key_sum[...] = jnp.zeros_like(key_sum)
    for mine in range(own):
        rows = slice(mine * slab, (mine + 1) * slab)
        for layer, (q_ref, g_ref) in enumerate(((q_first, g_first), (q_second, g_second))):
            for head in range(heads):
                at = (layer * heads + head) * slab
                cols = slice(head * HD, (head + 1) * HD)
                q_rows[mine, at : at + slab, :] = q_ref[rows, cols]
                g_rows[mine, at : at + slab, :] = g_ref[rows, cols]
    docs = doc_ref[...]
    bounds = [jnp.sum((docs <= i).astype(jnp.int32)) for i in range(3)]

    order_copy.wait()
    for i in range(slabs, PLACES):
        facts[i] = 0

    def invert(i, carried):
        facts[order_ref[i]] = i
        return carried

    lax.fori_loop(0, slabs, invert, 0)
    first_slab = lax.axis_index("ctx") * own

    def one_slab(mine, carried):
        pos0 = order_ref[first_slab + mine] * slab
        row_pos = pos0 + (lax.broadcasted_iota(jnp.int32, (1, HD), 1) & (slab - 1))
        row_doc = jnp.zeros((1, HD), jnp.int32)
        low = jnp.int32(0)
        for bound in bounds:
            row_doc = jnp.where(row_pos >= bound, bound, row_doc)
            low = jnp.where(pos0 >= bound, bound, low)
        low = low // slab
        out_rows = pl.ds(pl.multiple_of(mine * slab, slab), slab)

        def work(size):
            q, g = q_rows[mine], g_rows[mine]
            top = jnp.full((1, width), MASKED_SCORE, jnp.float32)
            norm = weighted = jnp.zeros((1, width), jnp.float32)
            for start, part in chunks(size):
                key_pos = low * slab + start + lax.broadcasted_iota(jnp.int32, (part, HD), 0)
                allowed = (key_pos <= row_pos) & (key_pos >= row_doc)
                allowed = jnp.concatenate([allowed] * (width // HD), axis=1)
                at = places(facts, low, start, part, slab)
                rows = slice(start, start + part)
                keys = jnp.concatenate([kv_ref[a, :HD] for a in at], axis=0)
                values = jnp.concatenate([kv_ref[a, HD:] for a in at], axis=0)
                s = jnp.where(allowed, dot(keys, q, NT) * scale2, MASKED_SCORE)
                scores_ref[rows, :] = s
                dp = dot(values, g, NT)
                grads_ref[rows, :] = dp
                new_top = jnp.maximum(top, jnp.max(s, axis=0, keepdims=True))
                e = jnp.exp2(s - new_top)
                fix = jnp.exp2(top - new_top)
                norm = norm * fix + jnp.sum(e, axis=0, keepdims=True)
                weighted = weighted * fix + jnp.sum(e * dp, axis=0, keepdims=True)
                top = new_top
            lse = top + jnp.log2(norm)
            delta = weighted / norm
            for start, part in chunks(size):
                at = places(facts, low, start, part, slab)
                rows = slice(start, start + part)
                p = jnp.exp2(scores_ref[rows, :] - lse)
                ds = (p * (grads_ref[rows, :] - delta)).astype(jnp.bfloat16)
                ds_ref[rows, :] = ds
                dv = dot(p.astype(jnp.bfloat16), g, NN)
                dk = dot(ds, q, NN)
                for j, a in enumerate(at):
                    piece = slice(j * slab, (j + 1) * slab)
                    key_sum[a, :HD] += dk[piece] * scale
                    key_sum[a, HD:] += dv[piece]
            at = places(facts, low, 0, size, slab)
            keys = jnp.concatenate([kv_ref[a, :HD] for a in at], axis=0)
            dq = (dot(keys.T, ds_ref[:size, :], NN) * scale).T.astype(jnp.bfloat16)
            for layer, out in enumerate((dq_first, dq_second)):
                for head in range(heads):
                    at = (layer * heads + head) * slab
                    out[out_rows, head * HD : (head + 1) * HD] = dq[at : at + slab, :]

        for_size(pos0 + slab - low * slab, work)
        return carried

    lax.fori_loop(0, own, one_slab, 0)
    kvg_ref[...] = key_sum[...].astype(jnp.bfloat16)


def attention(slab_order, doc_ids, q_first, q_second, g_first, g_second, kv):
    rows, width = q_first.shape
    slab = kv.shape[0] // slab_order.shape[0]
    own = rows // slab
    cols = 2 * (width // HD) * slab
    most = SIZES[-1]
    out = jax.ShapeDtypeStruct((rows, width), jnp.bfloat16)
    vmem = pl.BlockSpec(memory_space=pltpu.VMEM)
    return pl.pallas_call(
        attention_kernel,
        out_shape=(out, out, jax.ShapeDtypeStruct(kv.shape, jnp.bfloat16)),
        in_specs=[pl.BlockSpec(memory_space=pltpu.HBM)] + [vmem] * 6,
        out_specs=(vmem,) * 3,
        scratch_shapes=[
            pltpu.SMEM(slab_order.shape, jnp.int32),
            pltpu.SMEM((PLACES,), jnp.int32),
            pltpu.VMEM((own, cols, HD), jnp.bfloat16),
            pltpu.VMEM((own, cols, HD), jnp.bfloat16),
            pltpu.VMEM((most, cols), jnp.float32),
            pltpu.VMEM((most, cols), jnp.float32),
            pltpu.VMEM((most, cols), jnp.bfloat16),
            pltpu.VMEM(kv.shape, jnp.float32),
            pltpu.SemaphoreType.DMA(()),
        ],
        compiler_params=pltpu.CompilerParams(vmem_limit_bytes=32 * 1024 * 1024),
    )(slab_order, doc_ids.reshape(-1, HD), q_first, q_second, g_first, g_second, kv)


SIDE = 4
ALONG_X = [[x * SIDE + y for x in range(SIDE)] for y in range(SIDE)]
ALONG_Y = [[x * SIDE + y for y in range(SIDE)] for x in range(SIDE)]


def exchange(blocks, groups):
    return lax.all_to_all(blocks, "ctx", 0, 0, axis_index_groups=groups)


def spread(block, groups):
    copies = jnp.broadcast_to(block[None], (SIDE,) + block.shape)
    return exchange(copies, groups).reshape(SIDE * block.shape[0], block.shape[1])


def per_device(
    slab_order,
    doc_ids,
    query_first,
    query_second,
    shared_keys,
    shared_values,
    out_grad_first,
    out_grad_second,
):
    kv = jnp.concatenate([shared_keys, shared_values], axis=1)
    kv = spread(spread(kv, ALONG_Y), ALONG_X)
    dq_first, dq_second, terms = attention(
        slab_order, doc_ids, query_first, query_second, out_grad_first, out_grad_second, kv
    )
    parts = exchange(terms.reshape(SIDE, -1, 2 * HD), ALONG_X)
    summed = jnp.sum(parts.astype(jnp.float32), axis=0).astype(jnp.bfloat16)
    parts = exchange(summed.reshape(SIDE, -1, 2 * HD), ALONG_Y)
    dk = jnp.sum(parts[:, :, :HD].astype(jnp.float32), axis=0).astype(jnp.bfloat16)
    dv = jnp.sum(parts[:, :, HD:].astype(jnp.float32), axis=0).astype(jnp.bfloat16)
    return (dq_first, dq_second, dk, dv)


def solution(mesh):
    rows = P(("dp", "ctx"), "head")
    return jax.shard_map(
        per_device,
        mesh=mesh,
        in_specs=(P("dp"), P("dp")) + (rows,) * 6,
        out_specs=(rows,) * 4,
        check_vma=False,
    )
```

time: 79.8 us -> 75.5 us (0.946)
  blocking collectives: 32.3 us -> 66.4 us
  waiting for transfers between devices: 15.5 us -> 0 us
  starting transfers between devices: 13.2 us -> 0 us
  local copies, waits for them, and re-layouts: 7.45 us -> 0.74 us
  Pallas kernels: 7.71 us -> 5.59 us
    all_to_all x2 -> x4, blocking collectives: 32.3 us -> 66.4 us  [exchange(): return lax.all_to_all(blocks, 'ctx', 0, 0, axis_index_groups=groups)]
    all_to_all x2 -> x0, waiting for transfers between devices: 15.5 us -> none  [exchange(): return lax.all_to_all(blocks, 'ctx', 0, 0, axis_index_groups=groups)]
    all_to_all x2 -> x0, starting transfers between devices: 13.2 us -> none  [exchange(): return lax.all_to_all(blocks, 'ctx', 0, 0, axis_index_groups=groups)]
    unnamed x12, local copies, waits for them, and re-layouts: 6.39 us -> 0.66 us
    pallas_call x3 -> x1, Pallas kernels: 7.71 us -> 5.59 us  [attention(): pl.pallas_call(attention_kernel, out_shape=(out, out, jax.ShapeDtypeStruc...]
    broadcast_in_dim x2, local copies, waits for them, and re-layouts: 1.06 us -> 0.09 us  [spread(): copies = jnp.broadcast_to(block[None], (SIDE,) + block.shape)]
  transfers between devices with their start and end apart: 2 -> 0, of which waited for: 2 -> 0; matrix products, arithmetic and copies ran while one was open for 0% -> 0% of each run, Pallas kernels for 6% -> 0%
where the time goes in v4:
time: 75.5 us; the launch traced here: 75.2 us
  blocking collectives  66.4 us (88%)
  Pallas kernels  5.59 us (7%)
  other arithmetic  1.7 us (2%)
    all_to_all x4, blocking collectives, exchange(): return lax.all_to_all(blocks, 'ctx', 0, 0, axis_index_groups=groups)  66.4 us
    pallas_call x1, Pallas kernels, attention(): pl.pallas_call(attention_kernel, out_shape=(out, out, jax.ShapeDtypeStruc...  5.59 us

profile of v4, /device:TPU:448, one launch (start us, length us, event | category | flops | bytes accessed | tf_op | source)
XLA Modules:
  0.0 75.2 jit_solution(3073234348835543660)
XLA Ops:
  0.6 0.8 %pad_maximum_fusion = bf16[128,256]{1,0:T(8,128)(2,1)S(1)} fusion(bf16[128,128]{1,0:T(8,128)(2,1)} %param.13, bf16[128,128]{1,0:T(8,128)(2,1)} %param.12), kind=kLoop, calls=%fused_computation.2 | loop fusion | flops 131072 | bytes 131072 | tf_op jit(solution)/shard_map/concatenate | solution.py:210
  1.4 17.7 %all_to_all.20 = bf16[4,128,256]{2,1,0:T(8,128)(2,1)S(1)} all-to-all(bf16[4,128,256]{2,1,0:T(8,128)(2,1)S(1)} %broadcast_in_dim.6), channel_id=1, replica_groups={{0,1,2,3},{4,5,6,7},{8,9,10,11},{12,13,14,15},{16,17,18,19},{20,21,22,2..., dimensions={0} | all-to-all | bytes 524288 | tf_op jit(solution)/shard_map/all_to_all | solution.py:192
  19.2 0.1 broadcast_in_dim.15
  19.2 0.0 copy-start
  19.2 0.0 copy-start.1
  19.3 0.0 copy-start.2
  19.3 0.0 copy-start.3
  19.3 0.0 copy-start.4
  19.3 16.9 %all_to_all.21 = bf16[4,512,256]{2,1,0:T(8,128)(2,1)S(1)} all-to-all(bf16[4,512,256]{2,1,0:T(8,128)(2,1)S(1)} %broadcast_in_dim.15), channel_id=1, replica_groups={{0,4,8,12},{1,5,9,13},{2,6,10,14},{3,7,11,15},{16,20,24,28},{17,21,25,2..., dimensions={0} | all-to-all | bytes 2097152 | tf_op jit(solution)/shard_map/all_to_all | solution.py:192
  36.2 0.0 copy-start.5
  36.2 0.0 copy-done
  36.2 0.0 copy-done.1
  36.2 0.0 copy-done.2
  36.2 0.0 copy-done.3
  36.2 0.0 copy-done.4
  36.2 0.6 copy-done.5
  36.8 5.6 %shard_map.111 = (bf16[128,768]{1,0:T(8,128)(2,1)}, bf16[128,768]{1,0:T(8,128)(2,1)}, bf16[2048,256]{1,0:T(8,128)(2,1)S(1)}) custom-call(s32[32]{0:T(128)S(1)} %copy-done.5, s32[16,128]{1,0:T(8,128)S(1)} %bitcast.7, bf16[128,768]{1,0:T(8,128)(2,1)S(1)} %copy-done, bf16[128,768]{1,0:T(8,128)(2,1)S(1)} %copy-done.1, bf16[128,768]{1,0:T(8,128)(2,1)S(1)} %copy-done.2, ...), custom_call_target="tpu_custom_call" | custom-call | tf_op jit(solution)/shard_map/pallas_call | solution.py:166
  42.4 14.0 %all_to_all.22 = bf16[4,512,256]{2,1,0:T(8,128)(2,1)S(1)} all-to-all(bf16[4,512,256]{2,1,0:T(8,128)(2,1)S(1)} %bitcast.6), channel_id=1, replica_groups={{0,4,8,12},{1,5,9,13},{2,6,10,14},{3,7,11,15},{16,20,24,28},{17,21,25,2..., dimensions={0} | all-to-all | bytes 2097152 | tf_op jit(solution)/shard_map/all_to_all | solution.py:192
  56.4 0.3 reduce_sum.36
  56.7 17.8 %all_to_all.23 = bf16[4,128,256]{2,1,0:T(8,128)(2,1)S(1)} all-to-all(bf16[4,128,256]{2,1,0:T(8,128)(2,1)S(1)} %bitcast.8), channel_id=1, replica_groups={{0,1,2,3},{4,5,6,7},{8,9,10,11},{12,13,14,15},{16,17,18,19},{20,21,22,2..., dimensions={0} | all-to-all | bytes 524288 | tf_op jit(solution)/shard_map/all_to_all | solution.py:192
  74.5 0.7 slice_reduce_fusion
  (1 shorter events, 0.0 us)
Async XLA Ops:
  19.2 17.0 %copy-start = (bf16[128,768]{1,0:T(8,128)(2,1)S(1)}, bf16[128,768]{1,0:T(8,128)(2,1)}, u32[]{:S(2)}) copy-start(bf16[128,768]{1,0:T(8,128)(2,1)} %q_first.1) | copy-start | bytes 589828
  19.2 16.9 %copy-start.1 = (bf16[128,768]{1,0:T(8,128)(2,1)S(1)}, bf16[128,768]{1,0:T(8,128)(2,1)}, u32[]{:S(2)}) copy-start(bf16[128,768]{1,0:T(8,128)(2,1)} %q_second.1) | copy-start | bytes 589828
  19.3 16.9 %copy-start.2 = (bf16[128,768]{1,0:T(8,128)(2,1)S(1)}, bf16[128,768]{1,0:T(8,128)(2,1)}, u32[]{:S(2)}) copy-start(bf16[128,768]{1,0:T(8,128)(2,1)} %g_first.1) | copy-start | bytes 589828
  19.3 16.9 %copy-start.3 = (bf16[128,768]{1,0:T(8,128)(2,1)S(1)}, bf16[128,768]{1,0:T(8,128)(2,1)}, u32[]{:S(2)}) copy-start(bf16[128,768]{1,0:T(8,128)(2,1)} %g_second.1) | copy-start | bytes 589828
  19.3 16.9 %copy-start.4 = (s32[2048]{0:T(1024)S(1)}, s32[2048]{0:T(1024)}, u32[]{:S(2)}) copy-start(s32[2048]{0:T(1024)} %param.9) | copy-start | bytes 24580
  36.2 0.7 copy-start.5

commit v5 on v3

--- a/solution.py
+++ b/solution.py
@@ -79,36 +79,40 @@
     return [(start, min(CHUNK, size - start)) for start in range(0, size, CHUNK)]
 
 
+def score_blocks(facts, mine, slab, size, kv_ref, q, g):
+    pos0, low, _ = key_range(facts, mine, slab)
+    row_pos = pos0 + (lax.broadcasted_iota(jnp.int32, (1, HD), 1) & (slab - 1))
+    row_doc = jnp.zeros((1, HD), jnp.int32)
+    for i in range(3):
+        row_doc = jnp.where(row_pos >= facts[FACTS + i], facts[FACTS + i], row_doc)
+    scale2 = math.log2(math.e) / math.sqrt(HD)
+    for start, part in chunks(size):
+        key_pos = low * slab + start + lax.broadcasted_iota(jnp.int32, (part, HD), 0)
+        allowed = (key_pos <= row_pos) & (key_pos >= row_doc)
+        allowed = jnp.concatenate([allowed] * (q.shape[0] // HD), axis=1)
+        at = places(facts, low, start, part, slab)
+        keys = jnp.concatenate([kv_ref[a, :HD] for a in at], axis=0)
+        values = jnp.concatenate([kv_ref[a, HD:] for a in at], axis=0)
+        s = jnp.where(allowed, dot(keys, q, NT) * scale2, MASKED_SCORE)
+        yield slice(start, start + part), at, keys, s, dot(values, g, NT)
+
+
 def main_kernel(
-    slab, facts, kv_ref, q_rows, g_rows, ds_ref, kvg_ref, scores_ref, grads_ref, key_sum
+    slab, facts, kv_ref, q_rows, g_rows, stats, kvg_ref, scores_ref, grads_ref, key_sum
 ):
     own, width, _ = q_rows.shape
     scale = 1.0 / math.sqrt(HD)
-    scale2 = scale * math.log2(math.e)
     key_sum[...] = jnp.zeros_like(key_sum)
 
     def one_slab(mine, carried):
-        pos0, low, need = key_range(facts, mine, slab)
-        row_pos = pos0 + (lax.broadcasted_iota(jnp.int32, (1, HD), 1) & (slab - 1))
-        row_doc = jnp.zeros((1, HD), jnp.int32)
-        for i in range(3):
-            row_doc = jnp.where(row_pos >= facts[FACTS + i], facts[FACTS + i], row_doc)
-
         def work(size):
             q, g = q_rows[mine], g_rows[mine]
             top = jnp.full((1, width), MASKED_SCORE, jnp.float32)
             norm = weighted = jnp.zeros((1, width), jnp.float32)
-            for start, part in chunks(size):
-                key_pos = low * slab + start + lax.broadcasted_iota(jnp.int32, (part, HD), 0)
-                allowed = (key_pos <= row_pos) & (key_pos >= row_doc)
-                allowed = jnp.concatenate([allowed] * (width // HD), axis=1)
-                at = places(facts, low, start, part, slab)
-                rows = slice(start, start + part)
-                keys = jnp.concatenate([kv_ref[a, :HD] for a in at], axis=0)
-                values = jnp.concatenate([kv_ref[a, HD:] for a in at], axis=0)
-                s = jnp.where(allowed, dot(keys, q, NT) * scale2, MASKED_SCORE)
+            blocks = []
+            for rows, at, _, s, dp in score_blocks(facts, mine, slab, size, kv_ref, q, g):
+                blocks.append((rows, at))
                 scores_ref[rows, :] = s
-                dp = dot(values, g, NT)
                 grads_ref[rows, :] = dp
                 new_top = jnp.maximum(top, jnp.max(s, axis=0, keepdims=True))
                 e = jnp.exp2(s - new_top)
@@ -118,12 +122,11 @@
                 top = new_top
             lse = top + jnp.log2(norm)
             delta = weighted / norm
-            for start, part in chunks(size):
-                at = places(facts, low, start, part, slab)
-                rows = slice(start, start + part)
+            stats[mine, 0:1, :] = lse
+            stats[mine, 1:2, :] = delta
+            for rows, at in blocks:
                 p = jnp.exp2(scores_ref[rows, :] - lse)
                 ds = (p * (grads_ref[rows, :] - delta)).astype(jnp.bfloat16)
-                ds_ref[mine, rows, :] = ds
                 dv = dot(p.astype(jnp.bfloat16), g, NN)
                 dk = dot(ds, q, NN)
                 for j, a in enumerate(at):
@@ -131,34 +134,37 @@
                     key_sum[a, :HD] += dk[piece] * scale
                     key_sum[a, HD:] += dv[piece]
 
-        for_size(need, work)
+        for_size(key_range(facts, mine, slab)[2], work)
         return carried
 
     lax.fori_loop(0, own, one_slab, 0)
     kvg_ref[...] = key_sum[...].astype(jnp.bfloat16)
 
 
-def query_kernel(facts, kv_ref, ds_ref, dq_first, dq_second):
-    own = ds_ref.shape[0]
+def query_kernel(facts, kv_ref, q_rows, g_rows, stats, dq_first, dq_second):
+    own, width, _ = q_rows.shape
     slab = dq_first.shape[0] // own
     heads = dq_first.shape[1] // HD
     scale = 1.0 / math.sqrt(HD)
 
     def one_slab(mine, carried):
-        _, low, need = key_range(facts, mine, slab)
-        rows = pl.ds(pl.multiple_of(mine * slab, slab), slab)
+        out_rows = pl.ds(pl.multiple_of(mine * slab, slab), slab)
 
         def work(size):
-            at = places(facts, low, 0, size, slab)
-            keys = jnp.concatenate([kv_ref[a, :HD] for a in at], axis=0)
-            dq = dot(keys.T, ds_ref[mine, :size, :], NN) * scale
-            dq = dq.T.astype(jnp.bfloat16)
+            lse, delta = stats[mine, 0:1, :], stats[mine, 1:2, :]
+            dq = jnp.zeros((HD, width), jnp.float32)
+            for _, _, keys, s, dp in score_blocks(
+                facts, mine, slab, size, kv_ref, q_rows[mine], g_rows[mine]
+            ):
+                ds = (jnp.exp2(s - lse) * (dp - delta)).astype(jnp.bfloat16)
+                dq = dq + dot(keys.T, ds, NN)
+            dq = (dq * scale).T.astype(jnp.bfloat16)
             for layer, out in enumerate((dq_first, dq_second)):
                 for head in range(heads):
                     at = (layer * heads + head) * slab
-                    out[rows, head * HD : (head + 1) * HD] = dq[at : at + slab, :]
-
-        for_size(need, work)
+                    out[out_rows, head * HD : (head + 1) * HD] = dq[at : at + slab, :]
+
+        for_size(key_range(facts, mine, slab)[2], work)
         return carried
 
     lax.fori_loop(0, own, one_slab, 0)
@@ -168,9 +174,12 @@
     return pl.CostEstimate(flops=flops, bytes_accessed=size, transcendentals=0)
 
 
+def room(mib):
+    return pltpu.CompilerParams(vmem_limit_bytes=mib * 1024 * 1024)
+
+
 VMEM = pl.BlockSpec(memory_space=pltpu.VMEM)
 SMEM = pl.BlockSpec(memory_space=pltpu.SMEM)
-ROOM = pltpu.CompilerParams(vmem_limit_bytes=40 * 1024 * 1024)
 
 
 def prepare(slab_order, doc_ids, q_first, q_second, g_first, g_second, own):
@@ -181,6 +190,7 @@
         out_shape=(stacked, stacked, jax.ShapeDtypeStruct((FACTS + 8,), jnp.int32)),
         in_specs=[SMEM] + [VMEM] * 5,
         out_specs=(VMEM, VMEM, SMEM),
+        compiler_params=room(4),
         cost_estimate=cost(0, 16 * rows * width),
     )(slab_order, doc_ids.reshape(-1, HD), q_first, q_second, g_first, g_second)
 
@@ -191,7 +201,7 @@
     return pl.pallas_call(
         functools.partial(main_kernel, slab),
         out_shape=(
-            jax.ShapeDtypeStruct((own, most, cols), jnp.bfloat16),
+            jax.ShapeDtypeStruct((own, 8, cols), jnp.float32),
             jax.ShapeDtypeStruct(kv.shape, jnp.bfloat16),
         ),
         in_specs=[SMEM] + [VMEM] * 3,
@@ -201,21 +211,22 @@
             pltpu.VMEM((most, cols), jnp.float32),
             pltpu.VMEM(kv.shape, jnp.float32),
         ],
-        compiler_params=ROOM,
-        cost_estimate=cost(8 * own * most * cols * HD, 4 * own * most * cols),
+        compiler_params=room(24),
+        cost_estimate=cost(8 * own * most * cols * HD, 4 * kv.size),
     )(facts, kv, q_rows, g_rows)
 
 
-def query_grads(facts, kv, ds, rows, width):
+def query_grads(facts, kv, q_rows, g_rows, stats, rows, width):
+    own, cols, _ = q_rows.shape
     out = jax.ShapeDtypeStruct((rows, width), jnp.bfloat16)
     return pl.pallas_call(
         query_kernel,
         out_shape=(out, out),
-        in_specs=[SMEM] + [VMEM] * 2,
+        in_specs=[SMEM] + [VMEM] * 4,
         out_specs=(VMEM,) * 2,
-        compiler_params=ROOM,
-        cost_estimate=cost(2 * ds.size * HD, 2 * ds.size),
-    )(facts, kv, ds)
+        compiler_params=room(20),
+        cost_estimate=cost(6 * own * SIZES[-1] * cols * HD, 4 * kv.size),
+    )(facts, kv, q_rows, g_rows, stats)
 
 
 SIDE = 4
@@ -246,12 +257,14 @@
     slab = rows * lax.axis_size("ctx") // slab_order.shape[0]
     own = rows // slab
     kv = jnp.concatenate([shared_keys, shared_values], axis=1)
-    kv = spread(spread(kv, ALONG_Y), ALONG_X)
-    q_rows, g_rows, facts = prepare(
+    kv = spread(kv, ALONG_Y)
+    ready = prepare(
         slab_order, doc_ids, query_first, query_second, out_grad_first, out_grad_second, own
     )
-    ds, terms = key_terms(facts, kv, q_rows, g_rows, slab)
-    dq_first, dq_second = query_grads(facts, kv, ds, rows, width)
+    kv, q_rows, g_rows, facts = lax.optimization_barrier((kv, *ready))
+    kv = spread(kv, ALONG_X)
+    stats, terms = key_terms(facts, kv, q_rows, g_rows, slab)
+    dq_first, dq_second = query_grads(facts, kv, q_rows, g_rows, stats, rows, width)
     parts = exchange(terms.reshape(SIDE, -1, 2 * HD), ALONG_X)
     summed = jnp.sum(parts.astype(jnp.float32), axis=0).astype(jnp.bfloat16)
     parts = exchange(summed.reshape(SIDE, -1, 2 * HD), ALONG_Y)

time: 79.8 us -> 75.2 us (0.942)
  local copies, waits for them, and re-layouts: 7.45 us -> 1.42 us
  starting transfers between devices: 13.2 us -> 16.7 us
  blocking collectives: 32.3 us -> 29.9 us
  Pallas kernels: 7.71 us -> 9.29 us
  waiting for transfers between devices: 15.5 us -> 14.4 us
    unnamed x12, local copies, waits for them, and re-layouts: 6.39 us -> 0.64 us
    all_to_all x2, starting transfers between devices: 13.2 us -> 16.7 us  [exchange(): return lax.all_to_all(blocks, 'ctx', 0, 0, axis_index_groups=groups)]
    all_to_all x2, blocking collectives: 32.3 us -> 29.9 us  [exchange(): return lax.all_to_all(blocks, 'ctx', 0, 0, axis_index_groups=groups)]
    pallas_call x1, Pallas kernels: 2.07 us -> 3.49 us  [query_grads(): pl.pallas_call(query_kernel, out_shape=(out, out), in_specs=[SMEM] + [VME...]
    pallas_call x1, Pallas kernels: 3.1 us -> 4.21 us  [key_terms(): pl.pallas_call(functools.partial(main_kernel, slab), out_shape=(jax.Shape...]
    all_to_all x2, waiting for transfers between devices: 15.5 us -> 14.4 us  [exchange(): return lax.all_to_all(blocks, 'ctx', 0, 0, axis_index_groups=groups)]
    pallas_call x1, Pallas kernels: 2.55 us -> 1.59 us  [prepare(): pl.pallas_call(prepare_kernel, out_shape=(stacked, stacked, jax.ShapeDtyp...]
  transfers between devices with their start and end apart: 2 -> 2, of which waited for: 2 -> 2; matrix products, arithmetic and copies ran while one was open for 0% -> 0% of each run, Pallas kernels for 6% -> 7%
where the time goes in v5:
time: 75.2 us; the launch traced here: 74.8 us
  blocking collectives  29.9 us (40%)
  starting transfers between devices  16.7 us (22%)
  waiting for transfers between devices  14.4 us (19%)
  Pallas kernels  9.29 us (12%)
  other arithmetic  2.34 us (3%)
  local copies, waits for them, and re-layouts  1.42 us (2%)
    all_to_all x2, blocking collectives, exchange(): return lax.all_to_all(blocks, 'ctx', 0, 0, axis_index_groups=groups)  29.9 us
    all_to_all x2, starting transfers between devices, exchange(): return lax.all_to_all(blocks, 'ctx', 0, 0, axis_index_groups=groups)  16.7 us
    all_to_all x2, waiting for transfers between devices, exchange(): return lax.all_to_all(blocks, 'ctx', 0, 0, axis_index_groups=groups)  14.4 us
    pallas_call x1, Pallas kernels, key_terms(): pl.pallas_call(functools.partial(main_kernel, slab), out_shape=(jax.Shape...  4.21 us
    pallas_call x1, Pallas kernels, query_grads(): pl.pallas_call(query_kernel, out_shape=(out, out), in_specs=[SMEM] + [VME...  3.49 us
    pallas_call x1, Pallas kernels, prepare(): pl.pallas_call(prepare_kernel, out_shape=(stacked, stacked, jax.ShapeDtyp...  1.59 us
  transfers between devices with their start and end apart: 2, of which 2 were waited for; matrix products, arithmetic and copies ran while one was open for 0% of the time, Pallas kernels for 7%

profile of v5, /device:TPU:448, one launch (start us, length us, event | category | flops | bytes accessed | tf_op | source)
XLA Modules:
  0.0 74.8 jit_solution(4446986935310781380)
XLA Ops:
  0.6 0.8 %pad_maximum_fusion = bf16[128,256]{1,0:T(8,128)(2,1)S(1)} fusion(bf16[128,128]{1,0:T(8,128)(2,1)} %param.13, bf16[128,128]{1,0:T(8,128)(2,1)} %param.12), kind=kLoop, calls=%fused_computation.2 | loop fusion | flops 131072 | bytes 131072 | tf_op jit(solution)/shard_map/concatenate | solution.py:259
  1.4 0.0 copy-start.2
  1.4 0.0 copy-start.3
  1.4 0.7 broadcast_in_dim.4
  2.2 0.0 copy-start
  2.2 0.0 copy-start.1
  2.2 7.2 %all-to-all-start = ((bf16[4,128,256]{2,1,0:T(8,128)(2,1)}), bf16[4,128,256]{2,1,0:T(8,128)(2,1)S(1)}, u32[]{:S(2)}, u32[]{:S(2)}) async-start(bf16[4,128,256]{2,1,0:T(8,128)(2,1)} %broadcast_in_dim.4), calls=%async_computation | async-start | bytes 524288 | tf_op jit(solution)/shard_map/all_to_all | solution.py:238
  9.4 0.0 copy-done.2
  9.4 0.0 copy-done.3
  9.4 0.0 copy-done
  9.4 0.0 copy-done.1
  9.4 0.0 copy-done.4
  9.4 0.6 copy-done.5
  10.0 1.6 %shard_map.111 = (bf16[2,768,128]{2,1,0:T(8,128)(2,1)S(1)}, bf16[2,768,128]{2,1,0:T(8,128)(2,1)S(1)}, s32[56]{0:T(128)S(1)}) custom-call(s32[32]{0:T(128)S(1)} %copy-done.5, s32[16,128]{1,0:T(8,128)S(1)} %bitcast.8, bf16[128,768]{1,0:T(8,128)(2,1)S(1)} %copy-done, bf16[128,768]{1,0:T(8,128)(2,1)S(1)} %copy-done.1, bf16[128,768]{1,0:T(8,128)(2,1)S(1)} %copy-done.2, ...), custom_call_target="tpu_custom_call" | custom-call | bytes 1572864 | tf_op jit(solution)/shard_map/pallas_call | solution.py:188
  11.6 8.2 %all-to-all-done = bf16[4,128,256]{2,1,0:T(8,128)(2,1)S(1)} async-done(((bf16[4,128,256]{2,1,0:T(8,128)(2,1)}), bf16[4,128,256]{2,1,0:T(8,128)(2,1)S(1)}, u32[]{:S(2)}, u32[]{:S(2)}) %all-to-all-start) | async-done | bytes 262176 | tf_op jit(solution)/shard_map/all_to_all | solution.py:238
  19.8 0.1 broadcast_in_dim.5
  19.9 16.6 %all_to_all.20 = bf16[4,512,256]{2,1,0:T(8,128)(2,1)S(1)} all-to-all(bf16[4,512,256]{2,1,0:T(8,128)(2,1)S(1)} %broadcast_in_dim.5), channel_id=1, replica_groups={{0,4,8,12},{1,5,9,13},{2,6,10,14},{3,7,11,15},{16,20,24,28},{17,21,25,2..., dimensions={0} | all-to-all | bytes 2097152 | tf_op jit(solution)/shard_map/all_to_all | solution.py:238
  36.5 4.2 %shard_map.112 = (f32[2,8,768]{2,1,0:T(8,128)S(1)}, bf16[2048,256]{1,0:T(8,128)(2,1)S(1)}) custom-call(s32[56]{0:T(128)S(1)} %get-tuple-element.18.facts, bf16[2048,256]{1,0:T(8,128)(2,1)S(1)} %bitcast.5, bf16[2,768,128]{2,1,0:T(8,128)(2,1)S(1)} %get-tuple-element.20.q_rows, bf16[2,768,128]{2,1,0:T(8,128)(2,1)S(1)} %get-tuple-element.21.g_rows), custom_call_target="tpu_custom_call" | custom-call | flops 1811939328 | bytes 2097152 | tf_op jit(solution)/shard_map/pallas_call | solution.py:201
  40.7 13.3 %all_to_all.21 = bf16[4,512,256]{2,1,0:T(8,128)(2,1)S(1)} all-to-all(bf16[4,512,256]{2,1,0:T(8,128)(2,1)S(1)} %bitcast.7), channel_id=1, replica_groups={{0,4,8,12},{1,5,9,13},{2,6,10,14},{3,7,11,15},{16,20,24,28},{17,21,25,2..., dimensions={0} | all-to-all | bytes 2097152 | tf_op jit(solution)/shard_map/all_to_all | solution.py:238
  54.0 0.9 %reduce_sum.36 = bf16[512,256]{1,0:T(8,128)(2,1)} reduce(bf16[4,512,256]{2,1,0:T(8,128)(2,1)S(1)} %all_to_all.21, bf16[]{:T(256)} %constant.4.clone.1), dimensions={0}, to_apply=%region_0.0 | reduce | flops 393216 | bytes 1310722 | tf_op jit(solution)/shard_map/reduce_sum | solution.py:269
  54.9 9.5 %all-to-all-start.3 = ((bf16[4,128,256]{2,1,0:T(8,128)(2,1)}), bf16[4,128,256]{2,1,0:T(8,128)(2,1)S(1)}, u32[]{:S(2)}, u32[]{:S(2)}) async-start(bf16[4,128,256]{2,1,0:T(8,128)(2,1)} %bitcast.4), calls=%async_computation.3 | async-start | bytes 524288 | tf_op jit(solution)/shard_map/all_to_all | solution.py:238
  64.4 3.5 %shard_map.113 = (bf16[128,768]{1,0:T(8,128)(2,1)}, bf16[128,768]{1,0:T(8,128)(2,1)}) custom-call(s32[56]{0:T(128)S(1)} %get-tuple-element.18.facts, bf16[2048,256]{1,0:T(8,128)(2,1)S(1)} %bitcast.6, bf16[2,768,128]{2,1,0:T(8,128)(2,1)S(1)} %get-tuple-element.20.q_rows, bf16[2,768,128]{2,1,0:T(8,128)(2,1)S(1)} %get-tuple-element.21.g_rows, ...), custom_call_target="tpu_custom_call" | custom-call | flops 1358954496 | bytes 2097152 | tf_op jit(solution)/shard_map/pallas_call | solution.py:222
  67.9 6.3 %all-to-all-done.3 = bf16[4,128,256]{2,1,0:T(8,128)(2,1)S(1)} async-done(((bf16[4,128,256]{2,1,0:T(8,128)(2,1)}), bf16[4,128,256]{2,1,0:T(8,128)(2,1)S(1)}, u32[]{:S(2)}, u32[]{:S(2)}) %all-to-all-start.3) | async-done | bytes 262176 | tf_op jit(solution)/shard_map/all_to_all | solution.py:238
  74.1 0.7 slice_reduce_fusion
  (2 shorter events, 0.0 us)
Async XLA Ops:
  1.4 8.0 %copy-start.2 = (bf16[128,768]{1,0:T(8,128)(2,1)S(1)}, bf16[128,768]{1,0:T(8,128)(2,1)}, u32[]{:S(2)}) copy-start(bf16[128,768]{1,0:T(8,128)(2,1)} %g_first.1) | copy-start | bytes 589828
  1.4 8.0 %copy-start.3 = (bf16[128,768]{1,0:T(8,128)(2,1)S(1)}, bf16[128,768]{1,0:T(8,128)(2,1)}, u32[]{:S(2)}) copy-start(bf16[128,768]{1,0:T(8,128)(2,1)} %g_second.1) | copy-start | bytes 589828
  2.2 7.2 %copy-start = (bf16[128,768]{1,0:T(8,128)(2,1)S(1)}, bf16[128,768]{1,0:T(8,128)(2,1)}, u32[]{:S(2)}) copy-start(bf16[128,768]{1,0:T(8,128)(2,1)} %q_first.1) | copy-start | bytes 589828
  2.2 7.3 %copy-start.1 = (bf16[128,768]{1,0:T(8,128)(2,1)S(1)}, bf16[128,768]{1,0:T(8,128)(2,1)}, u32[]{:S(2)}) copy-start(bf16[128,768]{1,0:T(8,128)(2,1)} %q_second.1) | copy-start | bytes 589828
  2.2 7.3 %copy-start.4 = (s32[2048]{0:T(1024)S(1)}, s32[2048]{0:T(1024)}, u32[]{:S(2)}) copy-start(s32[2048]{0:T(1024)} %param.9) | copy-start | bytes 24580
  2.2 17.7 %all-to-all-start = ((bf16[4,128,256]{2,1,0:T(8,128)(2,1)}), bf16[4,128,256]{2,1,0:T(8,128)(2,1)S(1)}, u32[]{:S(2)}, u32[]{:S(2)}) async-start(bf16[4,128,256]{2,1,0:T(8,128)(2,1)} %broadcast_in_dim.4), calls=%async_computation | async-start | bytes 524288 | tf_op jit(solution)/shard_map/all_to_all | solution.py:238
  9.4 0.7 copy-start.5
  54.9 19.2 %all-to-all-start.3 = ((bf16[4,128,256]{2,1,0:T(8,128)(2,1)}), bf16[4,128,256]{2,1,0:T(8,128)(2,1)S(1)}, u32[]{:S(2)}, u32[]{:S(2)}) async-start(bf16[4,128,256]{2,1,0:T(8,128)(2,1)} %bitcast.4), calls=%async_computation.3 | async-start | bytes 524288 | tf_op jit(solution)/shard_map/all_to_all | solution.py:238

commit v6 on v4

--- a/solution.py
+++ b/solution.py
@@ -9,7 +9,7 @@
 from jax.sharding import PartitionSpec as P
 
 HD = 128
-SIZES = (256, 512, 768, 1024, 1152)
+SIZES = (128, 256, 384, 512, 640, 768, 896, 1024, 1152)
 CHUNK = 512
 PLACES = 56
 MASKED_SCORE = -1e30
@@ -59,7 +59,9 @@
     grads_ref,
     ds_ref,
     key_sum,
+    dq_stage,
     order_sem,
+    dq_sems,
 ):
     slabs = order_ref.shape[0]
     own, width, _ = q_rows.shape
@@ -71,6 +73,8 @@
     order_copy.start()
 
     key_sum[...] = jnp.zeros_like(key_sum)
+    docs = doc_ref[...]
+    bounds = [jnp.sum((docs <= i).astype(jnp.int32)) for i in range(3)]
     for mine in range(own):
         rows = slice(mine * slab, (mine + 1) * slab)
         for layer, (q_ref, g_ref) in enumerate(((q_first, g_first), (q_second, g_second))):
@@ -79,19 +83,19 @@
                 cols = slice(head * HD, (head + 1) * HD)
                 q_rows[mine, at : at + slab, :] = q_ref[rows, cols]
                 g_rows[mine, at : at + slab, :] = g_ref[rows, cols]
-    docs = doc_ref[...]
-    bounds = [jnp.sum((docs <= i).astype(jnp.int32)) for i in range(3)]
-
     order_copy.wait()
     for i in range(slabs, PLACES):
         facts[i] = 0
-
-    def invert(i, carried):
+    for i in range(slabs):
         facts[order_ref[i]] = i
-        return carried
-
-    lax.fori_loop(0, slabs, invert, 0)
     first_slab = lax.axis_index("ctx") * own
+
+    def dq_copies(mine):
+        rows = pl.ds(pl.multiple_of(mine * slab, slab), slab)
+        return [
+            pltpu.make_async_copy(dq_stage.at[layer, rows], out.at[rows], dq_sems.at[mine, layer])
+            for layer, out in enumerate((dq_first, dq_second))
+        ]
 
     def one_slab(mine, carried):
         pos0 = order_ref[first_slab + mine] * slab
@@ -143,16 +147,22 @@
             at = places(facts, low, 0, size, slab)
             keys = jnp.concatenate([kv_ref[a, :HD] for a in at], axis=0)
             dq = (dot(keys.T, ds_ref[:size, :], NN) * scale).T.astype(jnp.bfloat16)
-            for layer, out in enumerate((dq_first, dq_second)):
+            for layer in range(2):
                 for head in range(heads):
                     at = (layer * heads + head) * slab
-                    out[out_rows, head * HD : (head + 1) * HD] = dq[at : at + slab, :]
+                    cols = slice(head * HD, (head + 1) * HD)
+                    dq_stage[layer, out_rows, cols] = dq[at : at + slab, :]
 
         for_size(pos0 + slab - low * slab, work)
+        for copy in dq_copies(mine):
+            copy.start()
         return carried
 
     lax.fori_loop(0, own, one_slab, 0)
     kvg_ref[...] = key_sum[...].astype(jnp.bfloat16)
+    for mine in range(own):
+        for copy in dq_copies(mine):
+            copy.wait()
 
 
 def attention(slab_order, doc_ids, q_first, q_second, g_first, g_second, kv):
@@ -163,11 +173,13 @@
     most = SIZES[-1]
     out = jax.ShapeDtypeStruct((rows, width), jnp.bfloat16)
     vmem = pl.BlockSpec(memory_space=pltpu.VMEM)
+    hbm = pl.BlockSpec(memory_space=pltpu.HBM)
+    slab_order = pltpu.with_memory_space_constraint(slab_order, pltpu.HBM)
     return pl.pallas_call(
         attention_kernel,
         out_shape=(out, out, jax.ShapeDtypeStruct(kv.shape, jnp.bfloat16)),
-        in_specs=[pl.BlockSpec(memory_space=pltpu.HBM)] + [vmem] * 6,
-        out_specs=(vmem,) * 3,
+        in_specs=[hbm] + [vmem] * 6,
+        out_specs=(hbm, hbm, vmem),
         scratch_shapes=[
             pltpu.SMEM(slab_order.shape, jnp.int32),
             pltpu.SMEM((PLACES,), jnp.int32),
@@ -177,7 +189,9 @@
             pltpu.VMEM((most, cols), jnp.float32),
             pltpu.VMEM((most, cols), jnp.bfloat16),
             pltpu.VMEM(kv.shape, jnp.float32),
+            pltpu.VMEM((2, rows, width), jnp.bfloat16),
             pltpu.SemaphoreType.DMA(()),
+            pltpu.SemaphoreType.DMA((own, 2)),
         ],
         compiler_params=pltpu.CompilerParams(vmem_limit_bytes=32 * 1024 * 1024),
     )(slab_order, doc_ids.reshape(-1, HD), q_first, q_second, g_first, g_second, kv)

time: 75.5 us -> 74.6 us (0.988)
  Pallas kernels: 5.59 us -> 4.81 us
    pallas_call x1, Pallas kernels: 5.59 us -> 4.81 us  [attention(): pl.pallas_call(attention_kernel, out_shape=(out, out, jax.ShapeDtypeStruc...]
where the time goes in v6:
time: 74.6 us; the launch traced here: 74.3 us
  blocking collectives  66.9 us (90%)
  Pallas kernels  4.81 us (6%)
  other arithmetic  1.7 us (2%)
    all_to_all x4, blocking collectives, exchange(): return lax.all_to_all(blocks, 'ctx', 0, 0, axis_index_groups=groups)  66.9 us
    pallas_call x1, Pallas kernels, attention(): pl.pallas_call(attention_kernel, out_shape=(out, out, jax.ShapeDtypeStruc...  4.81 us

profile of v6, /device:TPU:448, one launch (start us, length us, event | category | flops | bytes accessed | tf_op | source)
XLA Modules:
  0.0 74.3 jit_solution(11394863433013499467)
XLA Ops:
  0.6 0.8 %pad_maximum_fusion = bf16[128,256]{1,0:T(8,128)(2,1)S(1)} fusion(bf16[128,128]{1,0:T(8,128)(2,1)} %param.13, bf16[128,128]{1,0:T(8,128)(2,1)} %param.12), kind=kLoop, calls=%fused_computation.2 | loop fusion | flops 131072 | bytes 131072 | tf_op jit(solution)/shard_map/concatenate | solution.py:224
  1.4 17.7 %all_to_all.20 = bf16[4,128,256]{2,1,0:T(8,128)(2,1)S(1)} all-to-all(bf16[4,128,256]{2,1,0:T(8,128)(2,1)S(1)} %broadcast_in_dim.6), channel_id=1, replica_groups={{0,1,2,3},{4,5,6,7},{8,9,10,11},{12,13,14,15},{16,17,18,19},{20,21,22,2..., dimensions={0} | all-to-all | bytes 524288 | tf_op jit(solution)/shard_map/all_to_all | solution.py:206
  19.2 0.1 broadcast_in_dim.15
  19.2 0.0 copy-start
  19.2 0.0 copy-start.1
  19.3 0.0 copy-start.2
  19.3 0.0 copy-start.3
  19.3 0.0 copy-start.4
  19.3 16.9 %all_to_all.21 = bf16[4,512,256]{2,1,0:T(8,128)(2,1)S(1)} all-to-all(bf16[4,512,256]{2,1,0:T(8,128)(2,1)S(1)} %broadcast_in_dim.15), channel_id=1, replica_groups={{0,4,8,12},{1,5,9,13},{2,6,10,14},{3,7,11,15},{16,20,24,28},{17,21,25,2..., dimensions={0} | all-to-all | bytes 2097152 | tf_op jit(solution)/shard_map/all_to_all | solution.py:206
  36.2 0.0 copy-done
  36.2 0.0 copy-done.1
  36.2 0.0 copy-done.2
  36.2 0.0 copy-done.3
  36.2 0.0 copy-done.4
  36.2 4.8 %shard_map.111 = (bf16[128,768]{1,0:T(8,128)(2,1)}, bf16[128,768]{1,0:T(8,128)(2,1)}, bf16[2048,256]{1,0:T(8,128)(2,1)S(1)}) custom-call(s32[32]{0:T(128)} %order_hbm.1, s32[16,128]{1,0:T(8,128)S(1)} %bitcast.7, bf16[128,768]{1,0:T(8,128)(2,1)S(1)} %copy-done, bf16[128,768]{1,0:T(8,128)(2,1)S(1)} %copy-done.1, bf16[128,768]{1,0:T(8,128)(2,1)S(1)} %copy-done.2, ...), custom_call_target="tpu_custom_call" | custom-call | tf_op jit(solution)/shard_map/pallas_call | solution.py:178
  41.0 15.8 %all_to_all.22 = bf16[4,512,256]{2,1,0:T(8,128)(2,1)S(1)} all-to-all(bf16[4,512,256]{2,1,0:T(8,128)(2,1)S(1)} %bitcast.6), channel_id=1, replica_groups={{0,4,8,12},{1,5,9,13},{2,6,10,14},{3,7,11,15},{16,20,24,28},{17,21,25,2..., dimensions={0} | all-to-all | bytes 2097152 | tf_op jit(solution)/shard_map/all_to_all | solution.py:206
  56.9 0.3 reduce_sum.36
  57.1 16.5 %all_to_all.23 = bf16[4,128,256]{2,1,0:T(8,128)(2,1)S(1)} all-to-all(bf16[4,128,256]{2,1,0:T(8,128)(2,1)S(1)} %bitcast.8), channel_id=1, replica_groups={{0,1,2,3},{4,5,6,7},{8,9,10,11},{12,13,14,15},{16,17,18,19},{20,21,22,2..., dimensions={0} | all-to-all | bytes 524288 | tf_op jit(solution)/shard_map/all_to_all | solution.py:206
  73.6 0.7 slice_reduce_fusion
  (1 shorter events, 0.0 us)
Async XLA Ops:
  19.2 17.0 %copy-start = (bf16[128,768]{1,0:T(8,128)(2,1)S(1)}, bf16[128,768]{1,0:T(8,128)(2,1)}, u32[]{:S(2)}) copy-start(bf16[128,768]{1,0:T(8,128)(2,1)} %q_first.1) | copy-start | bytes 589828
  19.2 16.9 %copy-start.1 = (bf16[128,768]{1,0:T(8,128)(2,1)S(1)}, bf16[128,768]{1,0:T(8,128)(2,1)}, u32[]{:S(2)}) copy-start(bf16[128,768]{1,0:T(8,128)(2,1)} %q_second.1) | copy-start | bytes 589828
  19.3 16.9 %copy-start.2 = (bf16[128,768]{1,0:T(8,128)(2,1)S(1)}, bf16[128,768]{1,0:T(8,128)(2,1)}, u32[]{:S(2)}) copy-start(bf16[128,768]{1,0:T(8,128)(2,1)} %g_first.1) | copy-start | bytes 589828
  19.3 16.9 %copy-start.3 = (bf16[128,768]{1,0:T(8,128)(2,1)S(1)}, bf16[128,768]{1,0:T(8,128)(2,1)}, u32[]{:S(2)}) copy-start(bf16[128,768]{1,0:T(8,128)(2,1)} %g_second.1) | copy-start | bytes 589828
  19.3 16.9 %copy-start.4 = (s32[2048]{0:T(1024)S(1)}, s32[2048]{0:T(1024)}, u32[]{:S(2)}) copy-start(s32[2048]{0:T(1024)} %param.9) | copy-start | bytes 24580

commit v7 on v6

--- a/solution.py
+++ b/solution.py
@@ -10,7 +10,7 @@
 
 HD = 128
 SIZES = (128, 256, 384, 512, 640, 768, 896, 1024, 1152)
-CHUNK = 512
+CHUNK = 1152
 PLACES = 56
 MASKED_SCORE = -1e30
 NT = (((1,), (1,)), ((), ()))
@@ -32,7 +32,7 @@
 def places(facts, low, start, size, slab):
     first = low + start // slab
     return [
-        pl.ds(pl.multiple_of(facts[first + j] * slab, slab), slab) for j in range(size // slab)
+        pl.multiple_of(facts[first + j] * slab, slab) for j in range(size // slab)
     ]
 
 
@@ -87,7 +87,7 @@
     for i in range(slabs, PLACES):
         facts[i] = 0
     for i in range(slabs):
-        facts[order_ref[i]] = i
+        facts[order_ref[i]] = i // own * 2 * own + i % own
     first_slab = lax.axis_index("ctx") * own
 
     def dq_copies(mine):
@@ -118,8 +118,10 @@
                 allowed = jnp.concatenate([allowed] * (width // HD), axis=1)
                 at = places(facts, low, start, part, slab)
                 rows = slice(start, start + part)
-                keys = jnp.concatenate([kv_ref[a, :HD] for a in at], axis=0)
-                values = jnp.concatenate([kv_ref[a, HD:] for a in at], axis=0)
+                keys = jnp.concatenate([kv_ref[pl.ds(a, slab), :] for a in at], axis=0)
+                values = jnp.concatenate(
+                    [kv_ref[pl.ds(a + own * slab, slab), :] for a in at], axis=0
+                )
                 s = jnp.where(allowed, dot(keys, q, NT) * scale2, MASKED_SCORE)
                 scores_ref[rows, :] = s
                 dp = dot(values, g, NT)
@@ -142,10 +144,10 @@
                 dk = dot(ds, q, NN)
                 for j, a in enumerate(at):
                     piece = slice(j * slab, (j + 1) * slab)
-                    key_sum[a, :HD] += dk[piece] * scale
-                    key_sum[a, HD:] += dv[piece]
+                    key_sum[pl.ds(a, slab), :] += dk[piece] * scale
+                    key_sum[pl.ds(a + own * slab, slab), :] += dv[piece]
             at = places(facts, low, 0, size, slab)
-            keys = jnp.concatenate([kv_ref[a, :HD] for a in at], axis=0)
+            keys = jnp.concatenate([kv_ref[pl.ds(a, slab), :] for a in at], axis=0)
             dq = (dot(keys.T, ds_ref[:size, :], NN) * scale).T.astype(jnp.bfloat16)
             for layer in range(2):
                 for head in range(heads):
@@ -167,7 +169,7 @@
 
 def attention(slab_order, doc_ids, q_first, q_second, g_first, g_second, kv):
     rows, width = q_first.shape
-    slab = kv.shape[0] // slab_order.shape[0]
+    slab = kv.shape[0] // (2 * slab_order.shape[0])
     own = rows // slab
     cols = 2 * (width // HD) * slab
     most = SIZES[-1]
@@ -221,16 +223,17 @@
     out_grad_first,
     out_grad_second,
 ):
-    kv = jnp.concatenate([shared_keys, shared_values], axis=1)
+    kv = jnp.concatenate([shared_keys, shared_values], axis=0)
     kv = spread(spread(kv, ALONG_Y), ALONG_X)
     dq_first, dq_second, terms = attention(
         slab_order, doc_ids, query_first, query_second, out_grad_first, out_grad_second, kv
     )
-    parts = exchange(terms.reshape(SIDE, -1, 2 * HD), ALONG_X)
+    rows = shared_keys.shape[0]
+    parts = exchange(terms.reshape(SIDE, -1, HD), ALONG_X)
     summed = jnp.sum(parts.astype(jnp.float32), axis=0).astype(jnp.bfloat16)
-    parts = exchange(summed.reshape(SIDE, -1, 2 * HD), ALONG_Y)
-    dk = jnp.sum(parts[:, :, :HD].astype(jnp.float32), axis=0).astype(jnp.bfloat16)
-    dv = jnp.sum(parts[:, :, HD:].astype(jnp.float32), axis=0).astype(jnp.bfloat16)
+    parts = exchange(summed.reshape(SIDE, -1, HD), ALONG_Y)
+    dk = jnp.sum(parts[:, :rows].astype(jnp.float32), axis=0).astype(jnp.bfloat16)
+    dv = jnp.sum(parts[:, rows:].astype(jnp.float32), axis=0).astype(jnp.bfloat16)
     return (dq_first, dq_second, dk, dv)
 
 

time: 74.6 us -> 73.9 us (level)
  no operation moved by 1% of the time
where the time goes in v7:
time: 73.9 us; the launch traced here: 73.7 us
  blocking collectives  66.9 us (91%)
  Pallas kernels  4.14 us (6%)
  other arithmetic  1.71 us (2%)
    all_to_all x4, blocking collectives, exchange(): return lax.all_to_all(blocks, 'ctx', 0, 0, axis_index_groups=groups)  66.9 us
    pallas_call x1, Pallas kernels, attention(): pl.pallas_call(attention_kernel, out_shape=(out, out, jax.ShapeDtypeStruc...  4.14 us

profile of v7, /device:TPU:448, one launch (start us, length us, event | category | flops | bytes accessed | tf_op | source)
XLA Modules:
  0.0 73.7 jit_solution(331168447584589676)
XLA Ops:
  0.6 0.8 %pad_maximum_fusion = bf16[256,128]{1,0:T(8,128)(2,1)S(1)} fusion(bf16[128,128]{1,0:T(8,128)(2,1)} %param.13, bf16[128,128]{1,0:T(8,128)(2,1)} %param.12), kind=kLoop, calls=%fused_computation.2 | loop fusion | flops 131072 | bytes 131072 | tf_op jit(solution)/shard_map/concatenate | solution.py:226
  1.4 17.7 %all_to_all.20 = bf16[4,256,128]{2,1,0:T(8,128)(2,1)S(1)} all-to-all(bf16[4,256,128]{2,1,0:T(8,128)(2,1)S(1)} %broadcast_in_dim.6), channel_id=1, replica_groups={{0,1,2,3},{4,5,6,7},{8,9,10,11},{12,13,14,15},{16,17,18,19},{20,21,22,2..., dimensions={0} | all-to-all | bytes 524288 | tf_op jit(solution)/shard_map/all_to_all | solution.py:208
  19.2 0.1 broadcast_in_dim.15
  19.3 0.0 copy-start
  19.3 0.0 copy-start.1
  19.3 0.0 copy-start.2
  19.3 0.0 copy-start.3
  19.4 0.0 copy-start.4
  19.4 16.9 %all_to_all.21 = bf16[4,1024,128]{2,1,0:T(8,128)(2,1)S(1)} all-to-all(bf16[4,1024,128]{2,1,0:T(8,128)(2,1)S(1)} %broadcast_in_dim.15), channel_id=1, replica_groups={{0,4,8,12},{1,5,9,13},{2,6,10,14},{3,7,11,15},{16,20,24,28},{17,21,25,2..., dimensions={0} | all-to-all | bytes 2097152 | tf_op jit(solution)/shard_map/all_to_all | solution.py:208
  36.3 0.0 copy-done
  36.3 0.0 copy-done.1
  36.3 0.0 copy-done.2
  36.3 0.0 copy-done.3
  36.3 0.0 copy-done.4
  36.3 4.1 %shard_map.111 = (bf16[128,768]{1,0:T(8,128)(2,1)}, bf16[128,768]{1,0:T(8,128)(2,1)}, bf16[4096,128]{1,0:T(8,128)(2,1)S(1)}) custom-call(s32[32]{0:T(128)} %order_hbm.1, s32[16,128]{1,0:T(8,128)S(1)} %bitcast.7, bf16[128,768]{1,0:T(8,128)(2,1)S(1)} %copy-done, bf16[128,768]{1,0:T(8,128)(2,1)S(1)} %copy-done.1, bf16[128,768]{1,0:T(8,128)(2,1)S(1)} %copy-done.2, ...), custom_call_target="tpu_custom_call" | custom-call | tf_op jit(solution)/shard_map/pallas_call | solution.py:180
  40.4 14.9 %all_to_all.22 = bf16[4,1024,128]{2,1,0:T(8,128)(2,1)S(1)} all-to-all(bf16[4,1024,128]{2,1,0:T(8,128)(2,1)S(1)} %bitcast.6), channel_id=1, replica_groups={{0,4,8,12},{1,5,9,13},{2,6,10,14},{3,7,11,15},{16,20,24,28},{17,21,25,2..., dimensions={0} | all-to-all | bytes 2097152 | tf_op jit(solution)/shard_map/all_to_all | solution.py:208
  55.3 0.3 reduce_sum.36
  55.6 17.5 %all_to_all.23 = bf16[4,256,128]{2,1,0:T(8,128)(2,1)S(1)} all-to-all(bf16[4,256,128]{2,1,0:T(8,128)(2,1)S(1)} %bitcast.8), channel_id=1, replica_groups={{0,1,2,3},{4,5,6,7},{8,9,10,11},{12,13,14,15},{16,17,18,19},{20,21,22,2..., dimensions={0} | all-to-all | bytes 524288 | tf_op jit(solution)/shard_map/all_to_all | solution.py:208
  73.0 0.7 slice_reduce_fusion
  (1 shorter events, 0.0 us)
Async XLA Ops:
  19.3 17.0 %copy-start = (bf16[128,768]{1,0:T(8,128)(2,1)S(1)}, bf16[128,768]{1,0:T(8,128)(2,1)}, u32[]{:S(2)}) copy-start(bf16[128,768]{1,0:T(8,128)(2,1)} %q_first.1) | copy-start | bytes 589828
  19.3 16.9 %copy-start.1 = (bf16[128,768]{1,0:T(8,128)(2,1)S(1)}, bf16[128,768]{1,0:T(8,128)(2,1)}, u32[]{:S(2)}) copy-start(bf16[128,768]{1,0:T(8,128)(2,1)} %q_second.1) | copy-start | bytes 589828
  19.3 16.9 %copy-start.2 = (bf16[128,768]{1,0:T(8,128)(2,1)S(1)}, bf16[128,768]{1,0:T(8,128)(2,1)}, u32[]{:S(2)}) copy-start(bf16[128,768]{1,0:T(8,128)(2,1)} %g_first.1) | copy-start | bytes 589828
  19.3 16.9 %copy-start.3 = (bf16[128,768]{1,0:T(8,128)(2,1)S(1)}, bf16[128,768]{1,0:T(8,128)(2,1)}, u32[]{:S(2)}) copy-start(bf16[128,768]{1,0:T(8,128)(2,1)} %g_second.1) | copy-start | bytes 589828
  19.4 16.9 %copy-start.4 = (s32[2048]{0:T(1024)S(1)}, s32[2048]{0:T(1024)}, u32[]{:S(2)}) copy-start(s32[2048]{0:T(1024)} %param.9) | copy-start | bytes 24580

commit v8 on v7

--- a/solution.py
+++ b/solution.py
@@ -9,8 +9,8 @@
 from jax.sharding import PartitionSpec as P
 
 HD = 128
-SIZES = (128, 256, 384, 512, 640, 768, 896, 1024, 1152)
-CHUNK = 1152
+SIZES = (128, 256, 384, 512, 640, 768, 896, 1024, 1088)
+CHUNK = 1088
 PLACES = 56
 MASKED_SCORE = -1e30
 NT = (((1,), (1,)), ((), ()))

time: 73.9 us -> 75.2 us (1.018); the launches traced: 73.7 us -> 76 us
  blocking collectives: 66.9 us -> 69.9 us
    all_to_all x4, blocking collectives: 66.9 us -> 69.9 us  [exchange(): return lax.all_to_all(blocks, 'ctx', 0, 0, axis_index_groups=groups)]
where the time goes in v8:
time: 75.2 us; the launch traced here: 76 us
  blocking collectives  69.9 us (93%)
  Pallas kernels  3.5 us (5%)
  other arithmetic  1.71 us (2%)
    all_to_all x4, blocking collectives, exchange(): return lax.all_to_all(blocks, 'ctx', 0, 0, axis_index_groups=groups)  69.9 us
    pallas_call x1, Pallas kernels, attention(): pl.pallas_call(attention_kernel, out_shape=(out, out, jax.ShapeDtypeStruc...  3.5 us

profile of v8, /device:TPU:448, one launch (start us, length us, event | category | flops | bytes accessed | tf_op | source)
XLA Modules:
  0.0 76.0 jit_solution(11644825177598490443)
XLA Ops:
  0.6 0.8 %pad_maximum_fusion = bf16[256,128]{1,0:T(8,128)(2,1)S(1)} fusion(bf16[128,128]{1,0:T(8,128)(2,1)} %param.13, bf16[128,128]{1,0:T(8,128)(2,1)} %param.12), kind=kLoop, calls=%fused_computation.2 | loop fusion | flops 131072 | bytes 131072 | tf_op jit(solution)/shard_map/concatenate | solution.py:226
  1.4 17.7 %all_to_all.20 = bf16[4,256,128]{2,1,0:T(8,128)(2,1)S(1)} all-to-all(bf16[4,256,128]{2,1,0:T(8,128)(2,1)S(1)} %broadcast_in_dim.6), channel_id=1, replica_groups={{0,1,2,3},{4,5,6,7},{8,9,10,11},{12,13,14,15},{16,17,18,19},{20,21,22,2..., dimensions={0} | all-to-all | bytes 524288 | tf_op jit(solution)/shard_map/all_to_all | solution.py:208
  19.2 0.1 broadcast_in_dim.15
  19.3 0.0 copy-start
  19.3 0.0 copy-start.1
  19.3 0.0 copy-start.2
  19.3 0.0 copy-start.3
  19.4 0.0 copy-start.4
  19.4 16.9 %all_to_all.21 = bf16[4,1024,128]{2,1,0:T(8,128)(2,1)S(1)} all-to-all(bf16[4,1024,128]{2,1,0:T(8,128)(2,1)S(1)} %broadcast_in_dim.15), channel_id=1, replica_groups={{0,4,8,12},{1,5,9,13},{2,6,10,14},{3,7,11,15},{16,20,24,28},{17,21,25,2..., dimensions={0} | all-to-all | bytes 2097152 | tf_op jit(solution)/shard_map/all_to_all | solution.py:208
  36.3 0.0 copy-done
  36.3 0.0 copy-done.1
  36.3 0.0 copy-done.2
  36.3 0.0 copy-done.3
  36.3 0.0 copy-done.4
  36.3 3.5 %shard_map.111 = (bf16[128,768]{1,0:T(8,128)(2,1)}, bf16[128,768]{1,0:T(8,128)(2,1)}, bf16[4096,128]{1,0:T(8,128)(2,1)S(1)}) custom-call(s32[32]{0:T(128)} %order_hbm.1, s32[16,128]{1,0:T(8,128)S(1)} %bitcast.7, bf16[128,768]{1,0:T(8,128)(2,1)S(1)} %copy-done, bf16[128,768]{1,0:T(8,128)(2,1)S(1)} %copy-done.1, bf16[128,768]{1,0:T(8,128)(2,1)S(1)} %copy-done.2, ...), custom_call_target="tpu_custom_call" | custom-call | tf_op jit(solution)/shard_map/pallas_call | solution.py:180
  39.8 15.7 %all_to_all.22 = bf16[4,1024,128]{2,1,0:T(8,128)(2,1)S(1)} all-to-all(bf16[4,1024,128]{2,1,0:T(8,128)(2,1)S(1)} %bitcast.6), channel_id=1, replica_groups={{0,4,8,12},{1,5,9,13},{2,6,10,14},{3,7,11,15},{16,20,24,28},{17,21,25,2..., dimensions={0} | all-to-all | bytes 2097152 | tf_op jit(solution)/shard_map/all_to_all | solution.py:208
  55.5 0.3 reduce_sum.36
  55.7 19.6 %all_to_all.23 = bf16[4,256,128]{2,1,0:T(8,128)(2,1)S(1)} all-to-all(bf16[4,256,128]{2,1,0:T(8,128)(2,1)S(1)} %bitcast.8), channel_id=1, replica_groups={{0,1,2,3},{4,5,6,7},{8,9,10,11},{12,13,14,15},{16,17,18,19},{20,21,22,2..., dimensions={0} | all-to-all | bytes 524288 | tf_op jit(solution)/shard_map/all_to_all | solution.py:208
  75.3 0.7 slice_reduce_fusion
  (1 shorter events, 0.0 us)
Async XLA Ops:
  19.3 17.0 %copy-start = (bf16[128,768]{1,0:T(8,128)(2,1)S(1)}, bf16[128,768]{1,0:T(8,128)(2,1)}, u32[]{:S(2)}) copy-start(bf16[128,768]{1,0:T(8,128)(2,1)} %q_first.1) | copy-start | bytes 589828
  19.3 16.9 %copy-start.1 = (bf16[128,768]{1,0:T(8,128)(2,1)S(1)}, bf16[128,768]{1,0:T(8,128)(2,1)}, u32[]{:S(2)}) copy-start(bf16[128,768]{1,0:T(8,128)(2,1)} %q_second.1) | copy-start | bytes 589828
  19.3 16.9 %copy-start.2 = (bf16[128,768]{1,0:T(8,128)(2,1)S(1)}, bf16[128,768]{1,0:T(8,128)(2,1)}, u32[]{:S(2)}) copy-start(bf16[128,768]{1,0:T(8,128)(2,1)} %g_first.1) | copy-start | bytes 589828
  19.3 16.9 %copy-start.3 = (bf16[128,768]{1,0:T(8,128)(2,1)S(1)}, bf16[128,768]{1,0:T(8,128)(2,1)}, u32[]{:S(2)}) copy-start(bf16[128,768]{1,0:T(8,128)(2,1)} %g_second.1) | copy-start | bytes 589828
  19.4 16.9 %copy-start.4 = (s32[2048]{0:T(1024)S(1)}, s32[2048]{0:T(1024)}, u32[]{:S(2)}) copy-start(s32[2048]{0:T(1024)} %param.9) | copy-start | bytes 24580
